TPU v7x, 32 devices: a whole 2x2x4 slice. The times are simulated.
32 devices in a mesh: gy: 4 (over y, core), gz: 8 (over z, x).
Axes of the slice: x: 2, y: 2, z: 4, core: 2. Of those that a mesh axis runs over, the one named last changes fastest.
Arguments:
- linear_field: bfloat16 [3, 16, 64, 128], P(None, 'gy', 'gz'), may hold values from -6 to 6
- lift_kernel: bfloat16 [27, 32, 3], replicated, may hold values from -1 to 1
- fine_kernel: bfloat16 [27, 32, 32], replicated, may hold values from -0.3125 to 0.3125
- reduce_first: bfloat16 [8, 64, 32], replicated, may hold values from -0.5 to 0.5
- middle_kernel: bfloat16 [27, 64, 64], replicated, may hold values from -0.21875 to 0.21875
- reduce_second: bfloat16 [8, 128, 64], replicated, may hold values from -0.375 to 0.375
- coarse_kernel: bfloat16 [27, 128, 128], replicated, may hold values from -0.15625 to 0.15625
- expand_second: bfloat16 [8, 64, 128], replicated, may hold values from -0.75 to 0.75
- merge_middle: bfloat16 [27, 64, 128], replicated, may hold values from -0.15625 to 0.15625
- expand_first: bfloat16 [8, 32, 64], replicated, may hold values from -1 to 1
- merge_fine: bfloat16 [27, 32, 64], replicated, may hold values from -0.21875 to 0.21875
- output_head: bfloat16 [3, 32], replicated, may hold values from -1 to 1
Outputs:
- displacement: float32 [3, 16, 64, 128], P(None, 'gy', 'gz')
All inputs are finite; a program needn't handle non-finite values.
Results may differ from a plain program's by a relative error of at most 0.015.
Values may be sent and summed in bfloat16 or wider, within the bound.
No kernel may reach another device: no remote copies, remote signals or barrier semaphores. Data moves between devices by JAX's collectives and lax.ppermute only.
A program may use at most 64 MiB of HBM per device.

v0:
```python
import functools

import jax
import jax.numpy as jnp
import numpy as np
from jax import lax
from jax.experimental import pallas as pl
from jax.experimental.pallas import tpu as pltpu
from jax.sharding import PartitionSpec as P

BF = jnp.bfloat16
F32 = jnp.float32
VMEM = pl.BlockSpec(memory_space=pltpu.VMEM)
SMEM = pl.BlockSpec(memory_space=pltpu.SMEM)


def act(values):
    return jnp.maximum(values, 0.1 * values)


def dot(left, right):
    return jnp.dot(left, right, preferred_element_type=F32)


def split_fine():
    m = np.zeros((256, 256), np.float32)
    for row in range(2):
        for x in range(128):
            m[row * 128 + x, (x % 2) * 128 + row * 64 + x // 2] = 1
    return m


def split_middle():
    m = np.zeros((512, 512), np.float32)
    for row in range(4):
        for b in range(2):
            for x in range(64):
                m[row * 128 + b * 64 + x, (2 * b + x % 2) * 128 + row * 32 + x // 2] = 1
    return m


def coarse_taps():
    m = np.zeros((256, 9 * 128), np.float32)
    for dz in range(3):
        for dx in range(3):
            for row in range(4):
                for x in range(32):
                    m[(row + dz) * 32 + (x + dx - 1) % 32, (3 * dz + dx) * 128 + row * 32 + x] = 1
    return m


def lift_spread():
    m = np.zeros((81, 512), np.float32)
    for dy in range(3):
        for dz in range(3):
            for dx in range(3):
                for c in range(3):
                    m[(9 * dy + 3 * dz + dx) * 3 + c, ((dy * 3 + c) * 3 + dx) * 16 + dz] = 1
    return m


def prep_kernel(lift, fine, red1, mid, red2, mfine, spread, t_o, wf_o, wd1_o, wm_o, wd2_o, wmf_o):
    base = dot(lift[...], spread[...])
    for zo in range(8):
        moved = base if zo == 0 else pltpu.roll(base, zo, 1)
        t_o[32 * zo : 32 * zo + 32] = moved[:, :432].astype(BF)
    for dz in range(3):
        for dy in range(3):
            for dx in range(3):
                k = 3 * dy + dx
                wf_o[32 * dz : 32 * dz + 32, 32 * k : 32 * k + 32] = fine[9 * dy + 3 * dz + dx]
                wmf_o[32 * dz : 32 * dz + 32, 64 * k : 64 * k + 64] = mfine[9 * dy + 3 * dz + dx]
                j = 3 * dz + dx
                wm_o[64 * dy : 64 * dy + 64, 64 * j : 64 * j + 64] = mid[9 * dy + 3 * dz + dx]
    for t in range(8):
        wd1_o[:, 32 * t : 32 * t + 32] = red1[t]
        wd2_o[:, 64 * t : 64 * t + 64] = red2[t]


class Rows:
    def __init__(self, low, count, periodic):
        self.low, self.count, self.periodic = low, count, periodic

    def at(self, rel):
        if self.periodic:
            moved = rel - self.low + 4 * self.count
            return moved % self.count if isinstance(moved, int) else lax.rem(moved, self.count)
        return rel - self.low


def levels(periodic):
    if periodic:
        fine, mid, coarse = Rows(-8, 16, True), Rows(-4, 8, True), Rows(-2, 4, True)
        return fine, fine, fine, mid, mid, coarse
    return (
        Rows(-12, 28, False),
        Rows(-11, 26, False),
        Rows(-10, 24, False),
        Rows(-5, 12, False),
        Rows(-4, 10, False),
        Rows(-2, 5, False),
    )


def shifted_64(v, lane):
    edge_low = (lane % 64) == 0
    edge_high = (lane % 64) == 63
    low = jnp.where(edge_low, pltpu.roll(v, 65, 1), pltpu.roll(v, 1, 1))
    high = jnp.where(edge_high, pltpu.roll(v, 63, 1), pltpu.roll(v, 127, 1))
    return low, high


def net_kernel(
    periodic,
    me,
    lin,
    t_w,
    wf,
    wd1,
    wm,
    wd2,
    ck,
    we2,
    mmk,
    we1,
    wmf,
    head,
    s_fine,
    s_fine_t,
    s_mid,
    s_mid_t,
    s_taps,
    out,
    pat,
    lifted,
    fine,
    halves,
    mids,
    mskip,
    quarters,
    ctaps,
    ups,
    joined,
    mout,
    jfine,
):
    r_lin, r_lift, r_fine, r_mid, r_skip, r_coarse = levels(periodic)
    blocks = lin.shape[0]

    def patch(k, carry):
        block = lax.rem(me[0] + k // 4 + (blocks - 2), blocks) if periodic else k // 4
        for c in range(3):
            mid_v = lin[block, c, lax.rem(k, 4)].astype(F32)
            for dx, v in enumerate((pltpu.roll(mid_v, 1, 1), mid_v, pltpu.roll(mid_v, 127, 1))):
                v = jnp.concatenate([v, jnp.zeros((8, 128), F32)], axis=0)
                for j in range(4):
                    pat[k, j, (3 * c + dx) * 16 : (3 * c + dx) * 16 + 16] = v[8 * j : 8 * j + 16].astype(BF)
        return carry

    lax.fori_loop(0, r_lin.count, patch, 0)

    def lift(k, carry):
        rel = k + r_lift.low
        ys = [r_lin.at(rel + dy) for dy in (-1, 0, 1)]
        for pair in range(2):
            cols = [jnp.concatenate([pat[y, 2 * pair + h] for y in ys], axis=0) for h in range(2)]
            r = act(dot(t_w[...], jnp.concatenate(cols, axis=1)))
            for h in range(2):
                for zo in range(8):
                    z = 16 * pair + 8 * h + zo
                    if z < 30:
                        v = r[32 * zo : 32 * zo + 32, 128 * h : 128 * h + 128]
                        lifted[k, z, 0:32] = pltpu.roll(v, 1, 1).astype(BF)
                        lifted[k, z, 32:64] = v.astype(BF)
                        lifted[k, z, 64:96] = pltpu.roll(v, 127, 1).astype(BF)
        return carry

    lax.fori_loop(0, r_lift.count, lift, 0)

    def fine_conv(k, carry):
        rel = k + r_fine.low
        ys = [r_lift.at(rel + dy) for dy in (-1, 0, 1)]
        parts = []
        for pair in range(15):
            cols = [jnp.concatenate([lifted[y, 2 * pair + h] for y in ys], axis=0) for h in range(2)]
            r = dot(wf[...], jnp.concatenate(cols, axis=1))
            parts += [r[:, :128], r[:, 128:]]
        rows = []
        for z in range(28):
            v = parts[z][0:32] + parts[z + 1][32:64] + parts[z + 2][64:96]
            v = act(v).astype(BF)
            fine[k, z] = v
            rows.append(v)
        left = []
        for p in range(7):
            for b in range(2):
                left.append(jnp.concatenate([rows[4 * p + b], rows[4 * p + 2 + b]], axis=1))
        s = dot(jnp.concatenate(left, axis=0), s_fine[...]).astype(BF)
        for i in range(14):
            for c in range(2):
                halves[k, i // 2, (2 * (i % 2) + c) * 32 : (2 * (i % 2) + c) * 32 + 32] = s[
                    32 * i : 32 * i + 32, 128 * c : 128 * c + 128
                ]
        return carry

    lax.fori_loop(0, r_fine.count, fine_conv, 0)

    lane = lax.broadcasted_iota(jnp.int32, (64, 128), 1)

    def middle_in(k, carry):
        direct = [[], []]
        for p in range(7):
            cols = []
            for h in range(2):
                rel = 2 * (2 * k + h + r_mid.low)
                cols.append(jnp.concatenate([halves[r_fine.at(rel + a), p] for a in range(2)], axis=0))
            r = act(dot(wd1[...], jnp.concatenate(cols, axis=1)))
            for h in range(2):
                direct[h].append(r[:, 128 * h : 128 * h + 128])
        for h in range(2):
            turned = [pltpu.roll(v, 64, 1) for v in direct[h]]
            for pos in range(13):
                p = pos // 2
                v = direct[h][p] if pos % 2 == 0 else jnp.where(lane < 64, turned[p], turned[p + 1])
                low, high = shifted_64(v, lane)
                for dx, u in enumerate((low, v, high)):
                    at = pos * 192 + dx * 64
                    mids[2 * k + h, at : at + 64] = u.astype(BF)
        return carry

    lax.fori_loop(0, r_mid.count // 2, middle_in, 0)

    def middle_conv(k, carry):
        parts = []
        start = pl.multiple_of(k * 384, 384)
        for pair in range(r_mid.count // 2):
            cols = [mids[2 * pair + h, pl.ds(start, 576)] for h in range(2)]
            r = dot(wm[...], jnp.concatenate(cols, axis=1))
            parts += [r[:, :128], r[:, 128:]]
        for y in range(r_skip.count):
            rel = y + r_skip.low
            v = sum(parts[r_mid.at(rel + dy - 1)][64 * dy : 64 * dy + 64] for dy in range(3))
            mskip[y, k] = act(v).astype(BF)
        return carry

    lax.fori_loop(0, 6, middle_conv, 0)

    for chunk in range(2):
        width = 4 if chunk == 0 else 2
        left = [
            jnp.concatenate([mskip[y, 4 * chunk + q] for q in range(width)], axis=1) for y in range(r_skip.count)
        ]
        s = dot(jnp.concatenate(left, axis=0), s_mid[: 128 * width]).astype(BF)
        for y in range(r_skip.count):
            for t in range(4):
                quarters[y, t * 64 : t * 64 + 64, 128 * chunk : 128 * chunk + 128] = s[
                    64 * y : 64 * y + 64, 128 * t : 128 * t + 128
                ]
    for y in range(r_coarse.count):
        rel = 2 * (y + r_coarse.low)
        right = jnp.concatenate([quarters[r_skip.at(rel + a)] for a in range(2)], axis=0)
        cin = act(dot(wd2[...], right)).astype(BF)
        taps = dot(cin, s_taps[...]).astype(BF)
        for t in range(9):
            ctaps[y, 128 * t : 128 * t + 128] = taps[:, 128 * t : 128 * t + 128]

    wc = jnp.concatenate([ck[t] for t in range(27)], axis=1)
    for first in (-1, 1):
        rels = (first, first + 1) if first < 1 else (first, first)
        cols = [jnp.concatenate([ctaps[r_coarse.at(rel + dy)] for dy in (-1, 0, 1)], axis=0) for rel in rels]
        cout = act(dot(wc, jnp.concatenate(cols, axis=1))).astype(BF)
        u = act(dot(we2[...], cout)).astype(BF)
        for h in range(2 if first < 1 else 1):
            for a in range(2):
                left = jnp.concatenate(
                    [u[(4 * a + t) * 64 : (4 * a + t) * 64 + 64, 128 * h : 128 * h + 128] for t in range(4)], axis=1
                )
                s = dot(left, s_mid_t[...]).astype(BF)
                for q in range(4):
                    ups[2 * (first + 1 + h) + a, q] = s[:, 128 * q : 128 * q + 128]

    lane128 = lax.broadcasted_iota(jnp.int32, (128, 128), 1)
    for y in range(6):
        direct = [
            jnp.concatenate([ups[y, q], mskip[r_skip.at(y - 2), q + 1]], axis=0).astype(F32) for q in range(4)
        ]
        turned = [pltpu.roll(v, 64, 1) for v in direct]
        for pos in range(7):
            p = pos // 2
            v = direct[p] if pos % 2 == 0 else jnp.where(lane128 < 64, turned[p], turned[p + 1])
            low, high = shifted_64(v, lane128)
            for dx, u in enumerate((low, v, high)):
                at = pos * 384 + dx * 128
                joined[y, at : at + 128] = u.astype(BF)
    wmm = jnp.concatenate(
        [
            jnp.concatenate([mmk[9 * dy + 3 * dz + dx] for dz in range(3) for dx in range(3)], axis=1)
            for dy in range(3)
        ],
        axis=0,
    )
    for k in range(3):
        parts = []
        for pair in range(3):
            cols = [joined[2 * pair + h, 768 * k : 768 * k + 1152] for h in range(2)]
            r = dot(wmm, jnp.concatenate(cols, axis=1))
            parts += [r[:, :128], r[:, 128:]]
        for y in range(4):
            v = parts[y][0:64] + parts[y + 1][64:128] + parts[y + 2][128:192]
            mout[y, k] = act(v).astype(BF)

    for y in range(4):
        for k in range(3):
            u = act(dot(we1[...], mout[y, k])).astype(BF)
            left = []
            for ab in range(4):
                left.append(jnp.concatenate([u[64 * ab : 64 * ab + 32], u[64 * ab + 32 : 64 * ab + 64]], axis=1))
            s = dot(jnp.concatenate(left, axis=0), s_fine_t[...])
            for a in range(2):
                yf = 2 * (y - 1) + a
                if not -1 <= yf <= 4:
                    continue
                for b in range(2):
                    for h in range(2):
                        zf = -2 + 4 * k + 2 * h + b
                        if not -1 <= zf <= 8:
                            continue
                        up = s[(2 * a + b) * 32 : (2 * a + b) * 32 + 32, 128 * h : 128 * h + 128]
                        skip = fine[r_fine.at(yf), zf + 10].astype(F32)
                        v = jnp.concatenate([up, skip], axis=0)
                        jfine[yf + 1, zf + 1, 0:64] = pltpu.roll(v, 1, 1).astype(BF)
                        jfine[yf + 1, zf + 1, 64:128] = v.astype(BF)
                        jfine[yf + 1, zf + 1, 128:192] = pltpu.roll(v, 127, 1).astype(BF)

    for y in range(4):
        parts = []
        for pair in range(5):
            cols = [jnp.concatenate([jfine[y + dy, 2 * pair + h] for dy in range(3)], axis=0) for h in range(2)]
            r = dot(wmf[...], jnp.concatenate(cols, axis=1))
            parts += [r[:, :128], r[:, 128:]]
        rows = []
        for z in range(8):
            v = parts[z][0:32] + parts[z + 1][32:64] + parts[z + 2][64:96]
            rows.append(act(v).astype(BF))
        d = dot(head[...], jnp.concatenate(rows, axis=1))
        for z in range(8):
            for o in range(3):
                out[o, y, z : z + 1, :] = d[o : o + 1, 128 * z : 128 * z + 128]


def ring(axis, hops):
    count = lax.axis_size(axis)
    return [(i, (i + hops) % count) for i in range(count)]


def body(
    linear_field,
    lift_kernel,
    fine_kernel,
    reduce_first,
    middle_kernel,
    reduce_second,
    coarse_kernel,
    expand_second,
    merge_middle,
    expand_first,
    merge_fine,
    output_head,
):
    send = functools.partial(lax.ppermute, axis_name="gz")
    below = send(linear_field, perm=ring("gz", 1))
    above = send(linear_field, perm=ring("gz", -1))
    below_2 = send(linear_field[:, :, 4:], perm=ring("gz", 2))
    above_2 = send(linear_field[:, :, :4], perm=ring("gz", -2))
    wide = jnp.concatenate([below_2, below, linear_field, above, above_2], axis=2)
    count_y = lax.axis_size("gy")
    periodic = count_y == 4
    if periodic:
        lin = lax.all_gather(wide, "gy")
    else:
        lin = jnp.stack([wide if h == 0 else lax.ppermute(wide, "gy", ring("gy", -h)) for h in range(-3, 4)])
    me = lax.axis_index("gy").astype(jnp.int32).reshape(1)

    lift_flat = lift_kernel.transpose(1, 0, 2).reshape(32, 81)
    t_w, wf, wd1, wm, wd2, wmf = pl.pallas_call(
        prep_kernel,
        out_shape=[
            jax.ShapeDtypeStruct(s, BF)
            for s in ((256, 432), (96, 288), (64, 256), (192, 576), (128, 512), (96, 576))
        ],
        in_specs=[VMEM] * 7,
        out_specs=[VMEM] * 6,
        compiler_params=pltpu.CompilerParams(vmem_limit_bytes=16 << 20),
    )(lift_flat, fine_kernel, reduce_first, middle_kernel, reduce_second, merge_fine, lift_spread().astype(BF))

    r_lin, r_lift, r_fine, r_mid, r_skip, r_coarse = levels(periodic)
    split_f, split_m = split_fine().astype(BF), split_middle().astype(BF)
    head = jnp.pad(output_head, ((0, 13), (0, 0)))
    scratch = [
        pltpu.VMEM((r_lin.count, 4, 144, 128), BF),
        pltpu.VMEM((r_lift.count, 30, 96, 128), BF),
        pltpu.VMEM((r_fine.count, 28, 32, 128), BF),
        pltpu.VMEM((r_fine.count, 7, 128, 128), BF),
        pltpu.VMEM((r_mid.count, 13 * 192, 128), BF),
        pltpu.VMEM((r_skip.count, 6, 64, 128), BF),
        pltpu.VMEM((r_skip.count, 256, 256), BF),
        pltpu.VMEM((r_coarse.count, 1152, 128), BF),
        pltpu.VMEM((6, 4, 64, 128), BF),
        pltpu.VMEM((6, 7 * 384, 128), BF),
        pltpu.VMEM((4, 3, 64, 128), BF),
        pltpu.VMEM((6, 10, 192, 128), BF),
    ]
    return pl.pallas_call(
        functools.partial(net_kernel, periodic),
        out_shape=jax.ShapeDtypeStruct(linear_field.shape, F32),
        in_specs=[SMEM] + [VMEM] * 17,
        out_specs=VMEM,
        scratch_shapes=scratch,
        compiler_params=pltpu.CompilerParams(vmem_limit_bytes=56 << 20),
    )(
        me,
        lin,
        t_w,
        wf,
        wd1,
        wm,
        wd2,
        coarse_kernel,
        expand_second.reshape(512, 128),
        merge_middle,
        expand_first.reshape(256, 64),
        wmf,
        head,
        split_f,
        np.ascontiguousarray(split_f.T),
        split_m,
        np.ascontiguousarray(split_m.T),
        coarse_taps().astype(BF),
    )


def solution(mesh):
    return jax.shard_map(
        body,
        mesh=mesh,
        in_specs=(P(None, "gy", "gz", None), P(), P(), P(), P(), P(), P(), P(), P(), P(), P(), P()),
        out_specs=P(None, "gy", "gz", None),
        check_vma=False,
    )
```

profile of v0, /device:TPU:0, one launch (start us, length us, event | category | flops | bytes accessed | tf_op | source)
XLA Modules:
  0.0 66.0 jit_solution(16267731117429347663)
XLA Ops:
  0.0 0.0 copy-start
  0.0 2.9 %collective-permute-start.1 = (bf16[3,4,8,128]{3,2,1,0:T(8,128)(2,1)}, bf16[3,4,8,128]{3,2,1,0:T(8,128)(2,1)S(1)}, u32[]{:S(2)}, u32[]{:S(2)}) collective-permute-start(bf16[3,4,8,128]{3,2,1,0:T(8,128)(2,1)} %param.18), channel_id=1, source_target_pairs={{0,1},{1,2},{2,3},{3,4},{4,5},{5,6},{6,7},{7,0},{8,9},{9,10},{10,1... | collective-permute-start | bytes 73736 | tf_op jit(solution)/shard_map/ppermute | solution.py:371
  2.9 3.1 %collective-permute-start.2 = (bf16[3,4,8,128]{3,2,1,0:T(8,128)(2,1)}, bf16[3,4,8,128]{3,2,1,0:T(8,128)(2,1)S(1)}, u32[]{:S(2)}, u32[]{:S(2)}) collective-permute-start(bf16[3,4,8,128]{3,2,1,0:T(8,128)(2,1)} %param.18), channel_id=1, source_target_pairs={{0,7},{1,0},{2,1},{3,2},{4,3},{5,4},{6,5},{7,6},{8,15},{9,8},{10,9... | collective-permute-start | bytes 73736 | tf_op jit(solution)/shard_map/ppermute | solution.py:372
  6.0 0.8 %fusion = (bf16[3,4,4,128]{3,2,1,0:T(4,128)(2,1)S(1)}, bf16[3,4,4,128]{3,2,1,0:T(4,128)(2,1)S(1)}) fusion(bf16[3,4,8,128]{3,2,1,0:T(8,128)(2,1)} %param.18), kind=kLoop, calls=%fused_computation | loop fusion | bytes 49152 | tf_op jit(solution)/shard_map/slice | solution.py:374
  6.9 0.1 collective-permute-start
  6.9 3.8 %collective-permute-start.3 = (bf16[3,4,4,128]{3,2,1,0:T(4,128)(2,1)S(1)}, bf16[3,4,4,128]{3,2,1,0:T(4,128)(2,1)S(1)}, u32[]{:S(2)}, u32[]{:S(2)}) collective-permute-start(bf16[3,4,4,128]{3,2,1,0:T(4,128)(2,1)S(1)} %get-tuple-element.17), channel_id=1, source_target_pairs={{0,6},{1,7},{2,0},{3,1},{4,2},{5,3},{6,4},{7,5},{8,14},{9,15},{10,... | collective-permute-start | bytes 36872 | tf_op jit(solution)/shard_map/ppermute | solution.py:374
  10.7 0.0 copy-start.11
  10.7 1.1 %copy.29.red2 = bf16[8,128,64]{2,1,0:T(8,128)(2,1)S(1)} copy(bf16[8,128,64]{1,2,0:T(8,128)(2,1)} %param.23) | data formatting | bytes 262144 | tf_op args[5]
  11.8 0.0 copy-start.3
  11.8 1.0 %copy.28.red1 = bf16[8,64,32]{2,1,0:T(8,128)(2,1)S(1)} copy(bf16[8,64,32]{1,2,0:T(8,128)(2,1)} %param.21) | data formatting | bytes 65536 | tf_op args[3]
  12.8 0.0 copy-start.7
  12.8 0.0 copy-done.11
  12.9 0.1 copy.27.lift
  13.0 0.0 copy-start.12
  13.0 0.7 %copy-done.12 = bf16[3,32]{1,0:T(4,128)(2,1)S(1)} copy-done((bf16[3,32]{1,0:T(4,128)(2,1)S(1)}, bf16[3,32]{1,0:T(4,128)(2,1)}, u32[]{:S(2)}) %copy-start.12) | copy-done | bytes 216
  13.7 0.6 pad.4.head
  14.3 0.0 copy-done
  14.3 0.0 copy-done.3
  14.3 0.0 copy-done.7
  14.3 0.0 copy-start.4
  14.3 0.9 %copy-done.4 = bf16[27,32,64]{2,1,0:T(8,128)(2,1)S(1)} copy-done((bf16[27,32,64]{2,1,0:T(8,128)(2,1)S(1)}, bf16[27,32,64]{2,1,0:T(8,128)(2,1)}, u32[]{:S(2)}) %copy-start.4) | copy-done | bytes 110616
  15.2 0.0 copy-start.10
  15.2 0.5 shard_map.172
  15.8 0.0 copy-start.1
  15.8 0.7 %copy-done.1 = bf16[256,432]{1,0:T(8,128)(2,1)} copy-done((bf16[256,432]{1,0:T(8,128)(2,1)}, bf16[256,432]{1,0:T(8,128)(2,1)S(1)}, u32[]{:S(2)}) %copy-start.1) | copy-done | bytes 221208
  16.5 0.0 copy-start.2
  16.5 0.7 %copy-done.2 = bf16[192,576]{1,0:T(8,128)(2,1)} copy-done((bf16[192,576]{1,0:T(8,128)(2,1)}, bf16[192,576]{1,0:T(8,128)(2,1)S(1)}, u32[]{:S(2)}) %copy-start.2) | copy-done | bytes 221208
  17.2 0.0 copy-start.5
  17.2 0.7 copy-done.5
  17.8 0.0 copy-start.6
  17.8 0.6 copy-done.6
  18.5 0.0 copy-start.8
  18.5 0.6 copy-done.8
  19.1 0.0 copy-start.9
  19.1 0.6 copy-done.9
  19.7 0.0 collective-permute-done
  19.7 0.0 collective-permute-done.3
  19.7 0.0 collective-permute-done.1
  19.7 0.0 collective-permute-done.2
  19.7 0.0 copy-done.10
  19.7 0.5 concatenate.3
  20.3 7.1 %all-gather = bf16[12,4,32,128]{3,2,1,0:T(8,128)(2,1)} all-gather(bf16[3,4,32,128]{3,2,1,0:T(8,128)(2,1)S(1)} %concatenate.3), channel_id=2, replica_groups=mesh['gy'=4,'gz'=8] {'gy'}, dimensions={0}, use_global_device_ids=true | all-gather | bytes 491520 | tf_op jit(solution)/shard_map/all_gather | solution.py:379
  27.3 38.7 %shard_map.173 = f32[3,4,8,128]{3,2,1,0:T(8,128)} custom-call(s32[1]{0:T(128)} %bitcast.me, bf16[4,3,4,32,128]{4,3,2,1,0:T(8,128)(2,1)} %bitcast.7, bf16[256,432]{1,0:T(8,128)(2,1)} %copy-done.1, bf16[96,288]{1,0:T(8,128)(2,1)} %copy-done.8, bf16[64,256]{1,0:T(8,128)(2,1)} %copy-done.9, bf16[192,576]{1,0:T(8,128)(2,1)} %copy-done.2, ...), custom_call_target="tpu_custom_call" | custom-call | tf_op jit(solution)/shard_map/pallas_call | solution.py:413
  (2 shorter events, 0.0 us)
Async XLA Ops:
  0.0 14.3 %copy-start = (bf16[27,64,64]{2,1,0:T(8,128)(2,1)S(1)}, bf16[27,64,64]{2,1,0:T(8,128)(2,1)}, u32[]{:S(2)}) copy-start(bf16[27,64,64]{2,1,0:T(8,128)(2,1)} %mid.1) | copy-start | bytes 663556
  0.0 19.7 %collective-permute-start.1 = (bf16[3,4,8,128]{3,2,1,0:T(8,128)(2,1)}, bf16[3,4,8,128]{3,2,1,0:T(8,128)(2,1)S(1)}, u32[]{:S(2)}, u32[]{:S(2)}) collective-permute-start(bf16[3,4,8,128]{3,2,1,0:T(8,128)(2,1)} %param.18), channel_id=1, source_target_pairs={{0,1},{1,2},{2,3},{3,4},{4,5},{5,6},{6,7},{7,0},{8,9},{9,10},{10,1... | collective-permute-start | bytes 73736 | tf_op jit(solution)/shard_map/ppermute | solution.py:371
  2.9 16.8 %collective-permute-start.2 = (bf16[3,4,8,128]{3,2,1,0:T(8,128)(2,1)}, bf16[3,4,8,128]{3,2,1,0:T(8,128)(2,1)S(1)}, u32[]{:S(2)}, u32[]{:S(2)}) collective-permute-start(bf16[3,4,8,128]{3,2,1,0:T(8,128)(2,1)} %param.18), channel_id=1, source_target_pairs={{0,7},{1,0},{2,1},{3,2},{4,3},{5,4},{6,5},{7,6},{8,15},{9,8},{10,9... | collective-permute-start | bytes 73736 | tf_op jit(solution)/shard_map/ppermute | solution.py:372
  6.9 12.9 %collective-permute-start = (bf16[3,4,4,128]{3,2,1,0:T(4,128)(2,1)S(1)}, bf16[3,4,4,128]{3,2,1,0:T(4,128)(2,1)S(1)}, u32[]{:S(2)}, u32[]{:S(2)}) collective-permute-start(bf16[3,4,4,128]{3,2,1,0:T(4,128)(2,1)S(1)} %get-tuple-element.18), channel_id=1, source_target_pairs={{0,2},{1,3},{2,4},{3,5},{4,6},{5,7},{6,0},{7,1},{8,10},{9,11},{10,... | collective-permute-start | bytes 36872 | tf_op jit(solution)/shard_map/ppermute | solution.py:373
  6.9 12.8 %collective-permute-start.3 = (bf16[3,4,4,128]{3,2,1,0:T(4,128)(2,1)S(1)}, bf16[3,4,4,128]{3,2,1,0:T(4,128)(2,1)S(1)}, u32[]{:S(2)}, u32[]{:S(2)}) collective-permute-start(bf16[3,4,4,128]{3,2,1,0:T(4,128)(2,1)S(1)} %get-tuple-element.17), channel_id=1, source_target_pairs={{0,6},{1,7},{2,0},{3,1},{4,2},{5,3},{6,4},{7,5},{8,14},{9,15},{10,... | collective-permute-start | bytes 36872 | tf_op jit(solution)/shard_map/ppermute | solution.py:374
  10.7 2.1 %copy-start.11 = (bf16[27,32,3]{1,0,2:T(8,128)(2,1)S(1)}, bf16[27,32,3]{1,0,2:T(8,128)(2,1)}, u32[]{:S(2)}) copy-start(bf16[27,32,3]{1,0,2:T(8,128)(2,1)} %param.19) | copy-start | bytes 15556
  11.8 2.5 %copy-start.3 = (bf16[27,32,32]{2,1,0:T(8,128)(2,1)S(1)}, bf16[27,32,32]{2,1,0:T(8,128)(2,1)}, u32[]{:S(2)}) copy-start(bf16[27,32,32]{2,1,0:T(8,128)(2,1)} %fine.1) | copy-start | bytes 165892
  12.8 1.5 %copy-start.7 = (bf16[81,512]{1,0:T(8,128)(2,1)S(1)}, bf16[81,512]{1,0:T(8,128)(2,1)}, u32[]{:S(2)}) copy-start(bf16[81,512]{1,0:T(8,128)(2,1)} %constant.20.clone.spread) | copy-start | bytes 248836
  13.0 0.7 %copy-start.12 = (bf16[3,32]{1,0:T(4,128)(2,1)S(1)}, bf16[3,32]{1,0:T(4,128)(2,1)}, u32[]{:S(2)}) copy-start(bf16[3,32]{1,0:T(4,128)(2,1)} %param.29) | copy-start | bytes 580
  14.3 0.9 %copy-start.4 = (bf16[27,32,64]{2,1,0:T(8,128)(2,1)S(1)}, bf16[27,32,64]{2,1,0:T(8,128)(2,1)}, u32[]{:S(2)}) copy-start(bf16[27,32,64]{2,1,0:T(8,128)(2,1)} %mfine.1) | copy-start | bytes 331780
  15.2 4.5 %copy-start.10 = (bf16[3,4,8,128]{3,2,1,0:T(8,128)(2,1)S(1)}, bf16[3,4,8,128]{3,2,1,0:T(8,128)(2,1)}, u32[]{:S(2)}) copy-start(bf16[3,4,8,128]{3,2,1,0:T(8,128)(2,1)} %param.18) | copy-start | bytes 73732
  15.8 0.7 %copy-start.1 = (bf16[256,432]{1,0:T(8,128)(2,1)}, bf16[256,432]{1,0:T(8,128)(2,1)S(1)}, u32[]{:S(2)}) copy-start(bf16[256,432]{1,0:T(8,128)(2,1)S(1)} %get-tuple-element.11.t_w) | copy-start | bytes 663556
  16.5 0.7 %copy-start.2 = (bf16[192,576]{1,0:T(8,128)(2,1)}, bf16[192,576]{1,0:T(8,128)(2,1)S(1)}, u32[]{:S(2)}) copy-start(bf16[192,576]{1,0:T(8,128)(2,1)S(1)} %get-tuple-element.14.wm) | copy-start | bytes 663556
  17.2 0.7 copy-start.5
  17.8 0.7 copy-start.6
  18.5 0.6 copy-start.8
  19.1 0.6 copy-start.9
where the time goes:
time: 66.3 us; the launch traced here: 66 us
  Pallas kernels  39.2 us (59%)
  starting transfers between devices  9.9 us (15%)
  local copies, waits for them, and re-layouts  9.7 us (15%)
  blocking collectives  7.08 us (11%)
    pallas_call x1, Pallas kernels, body(): pl.pallas_call(functools.partial(net_kernel, periodic), out_shape=jax.Sha...  38.7 us
    unnamed x28, local copies, waits for them, and re-layouts  7.64 us
    all_gather x1, blocking collectives, body(): lin = lax.all_gather(wide, 'gy')  7.08 us
    ppermute x1, starting transfers between devices, body(): above_2 = send(linear_field[:, :, :4], perm=ring('gz', -2))  3.81 us
    ppermute x1, starting transfers between devices, body(): above = send(linear_field, perm=ring('gz', -1))  3.09 us
    ppermute x1, starting transfers between devices, body(): below = send(linear_field, perm=ring('gz', 1))  2.94 us
  transfers between devices with their start and end apart: 4, of which 0 were waited for; matrix products, arithmetic and copies ran while one was open for 5% of the time, Pallas kernels for 1%

commit v1 on v0

--- a/solution.py
+++ b/solution.py
@@ -2,7 +2,6 @@
 
 import jax
 import jax.numpy as jnp
-import numpy as np
 from jax import lax
 from jax.experimental import pallas as pl
 from jax.experimental.pallas import tpu as pltpu
@@ -11,6 +10,8 @@
 BF = jnp.bfloat16
 F32 = jnp.float32
 VMEM = pl.BlockSpec(memory_space=pltpu.VMEM)
+ANY = pl.BlockSpec(memory_space=pl.ANY)
+HBM = pl.BlockSpec(memory_space=pltpu.HBM)
 SMEM = pl.BlockSpec(memory_space=pltpu.SMEM)
 
 
@@ -22,59 +23,79 @@
     return jnp.dot(left, right, preferred_element_type=F32)
 
 
-def split_fine():
-    m = np.zeros((256, 256), np.float32)
-    for row in range(2):
-        for x in range(128):
-            m[row * 128 + x, (x % 2) * 128 + row * 64 + x // 2] = 1
-    return m
-
-
-def split_middle():
-    m = np.zeros((512, 512), np.float32)
-    for row in range(4):
-        for b in range(2):
-            for x in range(64):
-                m[row * 128 + b * 64 + x, (2 * b + x % 2) * 128 + row * 32 + x // 2] = 1
-    return m
-
-
-def coarse_taps():
-    m = np.zeros((256, 9 * 128), np.float32)
-    for dz in range(3):
-        for dx in range(3):
-            for row in range(4):
-                for x in range(32):
-                    m[(row + dz) * 32 + (x + dx - 1) % 32, (3 * dz + dx) * 128 + row * 32 + x] = 1
-    return m
-
-
-def lift_spread():
-    m = np.zeros((81, 512), np.float32)
-    for dy in range(3):
-        for dz in range(3):
-            for dx in range(3):
-                for c in range(3):
-                    m[(9 * dy + 3 * dz + dx) * 3 + c, ((dy * 3 + c) * 3 + dx) * 16 + dz] = 1
-    return m
-
-
-def prep_kernel(lift, fine, red1, mid, red2, mfine, spread, t_o, wf_o, wd1_o, wm_o, wd2_o, wmf_o):
-    base = dot(lift[...], spread[...])
+def iotas(rows, columns):
+    return (
+        lax.broadcasted_iota(jnp.int32, (rows, columns), 0),
+        lax.broadcasted_iota(jnp.int32, (rows, columns), 1),
+    )
+
+
+def chosen(test):
+    return jnp.where(test, 1.0, 0.0).astype(BF)
+
+
+def fine_order(i):
+    return ((i & 1) << 7) | ((i >> 7) << 6) | ((i & 127) >> 1)
+
+
+def middle_order(i):
+    return (((i >> 6) & 1) << 8) | ((i & 1) << 7) | ((i >> 7) << 5) | ((i & 63) >> 1)
+
+
+def coarse_tap(dz, dx):
+    r, c = iotas(256, 128)
+    return chosen(r == ((((c >> 5) + dz) << 5) | ((c + dx - 1) & 31)))
+
+
+def lift_spread(c):
+    r, col = iotas(27, 512)
+    return chosen(col == ((r // 9 * 3 + c) * 3 + r % 3) * 16 + r // 3 % 3)
+
+
+def prep_kernel(lift, *refs):
+    sources, refs = refs[:5], refs[5:]
+    results, refs = refs[:12], refs[12:]
+    (t_o, wf_o, wf9_o, wd1_o, wm_o, wd2_o, wmf_o, sf_o, sft_o, sm_o, smt_o, st_o), refs = refs[:12], refs[12:]
+    (fine, red1, mid, red2, mfine), sems, out_sems = refs[:5], refs[5], refs[6]
+    copies = [pltpu.make_async_copy(src, dst, sems.at[i]) for i, (src, dst) in enumerate(zip(sources, refs))]
+    for copy in copies:
+        copy.start()
+    r, c = iotas(256, 256)
+    sf_o[...] = chosen(fine_order(r) == c)
+    sft_o[...] = chosen(r == fine_order(c))
+    r, c = iotas(512, 512)
+    sm_o[...] = chosen(middle_order(r) == c)
+    smt_o[...] = chosen(r == middle_order(c))
+    for t in range(9):
+        st_o[:, 128 * t : 128 * t + 128] = coarse_tap(t // 3, t % 3)
+    base = sum(
+        lax.dot_general(lift[c], lift_spread(c), (((0,), (0,)), ((), ())), preferred_element_type=F32)
+        for c in range(3)
+    )
     for zo in range(8):
         moved = base if zo == 0 else pltpu.roll(base, zo, 1)
         t_o[32 * zo : 32 * zo + 32] = moved[:, :432].astype(BF)
+    for copy in copies:
+        copy.wait()
     for dz in range(3):
         for dy in range(3):
             for dx in range(3):
                 k = 3 * dy + dx
-                wf_o[32 * dz : 32 * dz + 32, 32 * k : 32 * k + 32] = fine[9 * dy + 3 * dz + dx]
+                if k < 8:
+                    wf_o[32 * dz : 32 * dz + 32, 32 * k : 32 * k + 32] = fine[9 * dy + 3 * dz + dx]
+                else:
+                    wf9_o[:, 32 * dz : 32 * dz + 32] = fine[9 * dy + 3 * dz + dx]
                 wmf_o[32 * dz : 32 * dz + 32, 64 * k : 64 * k + 64] = mfine[9 * dy + 3 * dz + dx]
                 j = 3 * dz + dx
                 wm_o[64 * dy : 64 * dy + 64, 64 * j : 64 * j + 64] = mid[9 * dy + 3 * dz + dx]
-    for t in range(8):
-        wd1_o[:, 32 * t : 32 * t + 32] = red1[t]
-        wd2_o[:, 64 * t : 64 * t + 64] = red2[t]
+    wd1_o[...] = red1[...].astype(F32).T.astype(BF)
+    wd2_o[...] = red2[...].astype(F32).T.astype(BF)
+    made = (t_o, wf_o, wf9_o, wd1_o, wm_o, wd2_o, wmf_o, sf_o, sft_o, sm_o, smt_o, st_o)
+    copies = [pltpu.make_async_copy(src, dst, out_sems.at[i]) for i, (src, dst) in enumerate(zip(made, results))]
+    for copy in copies:
+        copy.start()
+    for copy in copies:
+        copy.wait()
 
 
 class Rows:
@@ -103,54 +124,58 @@
 
 
 def shifted_64(v, lane):
-    edge_low = (lane % 64) == 0
-    edge_high = (lane % 64) == 63
+    edge_low = (lane & 63) == 0
+    edge_high = (lane & 63) == 63
     low = jnp.where(edge_low, pltpu.roll(v, 65, 1), pltpu.roll(v, 1, 1))
     high = jnp.where(edge_high, pltpu.roll(v, 63, 1), pltpu.roll(v, 127, 1))
     return low, high
 
 
-def net_kernel(
-    periodic,
-    me,
-    lin,
-    t_w,
-    wf,
-    wd1,
-    wm,
-    wd2,
-    ck,
-    we2,
-    mmk,
-    we1,
-    wmf,
-    head,
-    s_fine,
-    s_fine_t,
-    s_mid,
-    s_mid_t,
-    s_taps,
-    out,
-    pat,
-    lifted,
-    fine,
-    halves,
-    mids,
-    mskip,
-    quarters,
-    ctaps,
-    ups,
-    joined,
-    mout,
-    jfine,
-):
+def net_kernel(periodic, me, *refs):
+    count = 5 if periodic else 1
+    fields, refs = refs[:count], refs[count:]
+    head, weights, out, refs = refs[0], refs[1:17], refs[17], refs[18:]
+    pat, lifted, fine, halves, mskip, quarters, ctaps, ups, mout, joined = refs[:10]
+    held, sems = refs[10:26], refs[26]
+    near_by, field_sems = refs[27 : 27 + count], refs[27 + count]
+    field_copies = [
+        pltpu.make_async_copy(src, dst, field_sems.at[i]) for i, (src, dst) in enumerate(zip(fields, near_by))
+    ]
+    for copy in field_copies:
+        copy.start()
+    if periodic:
+        own, near, far, other_near, other_far = near_by
+    else:
+        wide = near_by[0]
+    copies = [pltpu.make_async_copy(src, dst, sems.at[i]) for i, (src, dst) in enumerate(zip(weights, held))]
+    for copy in copies:
+        copy.start()
+    (t_w, wf, wf9, wd1, wm, wd2, ck, we2, mmk, we1, wmf, s_fine, s_fine_t, s_mid, s_mid_t, s_taps) = held
+
+    def need(*names):
+        for name in names:
+            copies[[h is name for h in held].index(True)].wait()
+
     r_lin, r_lift, r_fine, r_mid, r_skip, r_coarse = levels(periodic)
-    blocks = lin.shape[0]
+    core = lax.rem(me[0], 2)
+
+    for copy in field_copies:
+        copy.wait()
 
     def patch(k, carry):
-        block = lax.rem(me[0] + k // 4 + (blocks - 2), blocks) if periodic else k // 4
+        row = lax.rem(k, 4)
+        if periodic:
+            block = lax.rem(me[0] + k // 4 + 2, 4)
         for c in range(3):
-            mid_v = lin[block, c, lax.rem(k, 4)].astype(F32)
+            if periodic:
+                mine = [ref[block, c, row].astype(F32) for ref in (near, far)]
+                others = [ref[block, c, row].astype(F32) for ref in (other_near, other_far)]
+                below_1, below_2 = (jnp.where(core == 0, m, t) for m, t in zip(mine, others))
+                above_1, above_2 = (jnp.where(core == 0, t, m) for m, t in zip(mine, others))
+                parts = [below_2[4:], below_1, own[block, c, row].astype(F32), above_1, above_2[:4]]
+                mid_v = jnp.concatenate(parts, axis=0)
+            else:
+                mid_v = wide[k // 4, c, row].astype(F32)
             for dx, v in enumerate((pltpu.roll(mid_v, 1, 1), mid_v, pltpu.roll(mid_v, 127, 1))):
                 v = jnp.concatenate([v, jnp.zeros((8, 128), F32)], axis=0)
                 for j in range(4):
@@ -158,6 +183,8 @@
         return carry
 
     lax.fori_loop(0, r_lin.count, patch, 0)
+
+    need(t_w)
 
     def lift(k, carry):
         rel = k + r_lift.low
@@ -170,27 +197,37 @@
                     z = 16 * pair + 8 * h + zo
                     if z < 30:
                         v = r[32 * zo : 32 * zo + 32, 128 * h : 128 * h + 128]
-                        lifted[k, z, 0:32] = pltpu.roll(v, 1, 1).astype(BF)
-                        lifted[k, z, 32:64] = v.astype(BF)
-                        lifted[k, z, 64:96] = pltpu.roll(v, 127, 1).astype(BF)
+                        lifted[k, 96 * z : 96 * z + 32] = pltpu.roll(v, 1, 1).astype(BF)
+                        lifted[k, 96 * z + 32 : 96 * z + 64] = v.astype(BF)
+                        lifted[k, 96 * z + 64 : 96 * z + 96] = pltpu.roll(v, 127, 1).astype(BF)
         return carry
 
-    lax.fori_loop(0, r_lift.count, lift, 0)
+    lax.fori_loop(0, r_lift.count, lift, 0, unroll=2)
+
+    need(wf, wf9, s_fine)
 
     def fine_conv(k, carry):
         rel = k + r_fine.low
         ys = [r_lift.at(rel + dy) for dy in (-1, 0, 1)]
         parts = []
         for pair in range(15):
-            cols = [jnp.concatenate([lifted[y, 2 * pair + h] for y in ys], axis=0) for h in range(2)]
+            cols = [
+                jnp.concatenate([*(lifted[y, 96 * (2 * pair + h) : 96 * (2 * pair + h) + 96] for y in ys[:2]), lifted[ys[2], 96 * (2 * pair + h) : 96 * (2 * pair + h) + 64]], axis=0)
+                for h in range(2)
+            ]
             r = dot(wf[...], jnp.concatenate(cols, axis=1))
             parts += [r[:, :128], r[:, 128:]]
         rows = []
-        for z in range(28):
-            v = parts[z][0:32] + parts[z + 1][32:64] + parts[z + 2][64:96]
-            v = act(v).astype(BF)
-            fine[k, z] = v
-            rows.append(v)
+        for pair in range(14):
+            last = [lifted[ys[2], 96 * (2 * pair + i) + 64 : 96 * (2 * pair + i) + 96] for i in range(4)]
+            cols = [jnp.concatenate(last[h : h + 3], axis=0) for h in range(2)]
+            r = dot(wf9[...], jnp.concatenate(cols, axis=1))
+            for h in range(2):
+                z = 2 * pair + h
+                v = parts[z][0:32] + parts[z + 1][32:64] + parts[z + 2][64:96] + r[:, 128 * h : 128 * h + 128]
+                v = act(v).astype(BF)
+                fine[k, z] = v
+                rows.append(v)
         left = []
         for p in range(7):
             for b in range(2):
@@ -203,9 +240,11 @@
                 ]
         return carry
 
-    lax.fori_loop(0, r_fine.count, fine_conv, 0)
+    lax.fori_loop(0, r_fine.count, fine_conv, 0, unroll=2)
 
     lane = lax.broadcasted_iota(jnp.int32, (64, 128), 1)
+
+    need(wd1)
 
     def middle_in(k, carry):
         direct = [[], []]
@@ -225,16 +264,18 @@
                 low, high = shifted_64(v, lane)
                 for dx, u in enumerate((low, v, high)):
                     at = pos * 192 + dx * 64
-                    mids[2 * k + h, at : at + 64] = u.astype(BF)
+                    lifted[2 * k + h, at : at + 64] = u.astype(BF)
         return carry
 
     lax.fori_loop(0, r_mid.count // 2, middle_in, 0)
+
+    need(wm)
 
     def middle_conv(k, carry):
         parts = []
         start = pl.multiple_of(k * 384, 384)
         for pair in range(r_mid.count // 2):
-            cols = [mids[2 * pair + h, pl.ds(start, 576)] for h in range(2)]
+            cols = [lifted[2 * pair + h, pl.ds(start, 576)] for h in range(2)]
             r = dot(wm[...], jnp.concatenate(cols, axis=1))
             parts += [r[:, :128], r[:, 128:]]
         for y in range(r_skip.count):
@@ -244,6 +285,8 @@
         return carry
 
     lax.fori_loop(0, 6, middle_conv, 0)
+
+    need(s_mid, wd2, s_taps)
 
     for chunk in range(2):
         width = 4 if chunk == 0 else 2
@@ -264,6 +307,8 @@
         for t in range(9):
             ctaps[y, 128 * t : 128 * t + 128] = taps[:, 128 * t : 128 * t + 128]
 
+    need(ck, we2, s_mid_t)
+
     wc = jnp.concatenate([ck[t] for t in range(27)], axis=1)
     for first in (-1, 1):
         rels = (first, first + 1) if first < 1 else (first, first)
@@ -278,6 +323,8 @@
                 s = dot(left, s_mid_t[...]).astype(BF)
                 for q in range(4):
                     ups[2 * (first + 1 + h) + a, q] = s[:, 128 * q : 128 * q + 128]
+
+    need(mmk)
 
     lane128 = lax.broadcasted_iota(jnp.int32, (128, 128), 1)
     for y in range(6):
@@ -309,6 +356,8 @@
             v = parts[y][0:64] + parts[y + 1][64:128] + parts[y + 2][128:192]
             mout[y, k] = act(v).astype(BF)
 
+    need(we1, s_fine_t)
+
     for y in range(4):
         for k in range(3):
             u = act(dot(we1[...], mout[y, k])).astype(BF)
@@ -328,14 +377,16 @@
                         up = s[(2 * a + b) * 32 : (2 * a + b) * 32 + 32, 128 * h : 128 * h + 128]
                         skip = fine[r_fine.at(yf), zf + 10].astype(F32)
                         v = jnp.concatenate([up, skip], axis=0)
-                        jfine[yf + 1, zf + 1, 0:64] = pltpu.roll(v, 1, 1).astype(BF)
-                        jfine[yf + 1, zf + 1, 64:128] = v.astype(BF)
-                        jfine[yf + 1, zf + 1, 128:192] = pltpu.roll(v, 127, 1).astype(BF)
+                        lifted[yf + 1, 192 * (zf + 1) + 0 : 192 * (zf + 1) + 64] = pltpu.roll(v, 1, 1).astype(BF)
+                        lifted[yf + 1, 192 * (zf + 1) + 64 : 192 * (zf + 1) + 128] = v.astype(BF)
+                        lifted[yf + 1, 192 * (zf + 1) + 128 : 192 * (zf + 1) + 192] = pltpu.roll(v, 127, 1).astype(BF)
+
+    need(wmf)
 
     for y in range(4):
         parts = []
         for pair in range(5):
-            cols = [jnp.concatenate([jfine[y + dy, 2 * pair + h] for dy in range(3)], axis=0) for h in range(2)]
+            cols = [jnp.concatenate([lifted[y + dy, 192 * (2 * pair + h) : 192 * (2 * pair + h) + 192] for dy in range(3)], axis=0) for h in range(2)]
             r = dot(wmf[...], jnp.concatenate(cols, axis=1))
             parts += [r[:, :128], r[:, 128:]]
         rows = []
@@ -367,61 +418,83 @@
     merge_fine,
     output_head,
 ):
-    send = functools.partial(lax.ppermute, axis_name="gz")
-    below = send(linear_field, perm=ring("gz", 1))
-    above = send(linear_field, perm=ring("gz", -1))
-    below_2 = send(linear_field[:, :, 4:], perm=ring("gz", 2))
-    above_2 = send(linear_field[:, :, :4], perm=ring("gz", -2))
-    wide = jnp.concatenate([below_2, below, linear_field, above, above_2], axis=2)
-    count_y = lax.axis_size("gy")
+    raw = [
+        fine_kernel,
+        reduce_first.transpose(0, 2, 1).reshape(256, 64),
+        middle_kernel,
+        reduce_second.transpose(0, 2, 1).reshape(512, 128),
+        merge_fine,
+    ]
+    forms = [
+        (256, 432),
+        (96, 256),
+        (32, 96),
+        (64, 256),
+        (192, 576),
+        (128, 512),
+        (96, 576),
+        (256, 256),
+        (256, 256),
+        (512, 512),
+        (512, 512),
+        (256, 1152),
+    ]
+    prepared = pl.pallas_call(
+        prep_kernel,
+        out_shape=[jax.ShapeDtypeStruct(s, BF) for s in forms],
+        in_specs=[VMEM] + [HBM] * len(raw),
+        out_specs=[HBM] * len(forms),
+        scratch_shapes=[pltpu.VMEM(s, BF) for s in forms]
+        + [pltpu.VMEM(w.shape, BF) for w in raw]
+        + [pltpu.SemaphoreType.DMA((len(raw),)), pltpu.SemaphoreType.DMA((len(forms),))],
+        cost_estimate=pl.CostEstimate(flops=4_000_000_000, bytes_accessed=10_000_000, transcendentals=0),
+        compiler_params=pltpu.CompilerParams(vmem_limit_bytes=60 << 20),
+    )(lift_kernel.transpose(2, 0, 1), *raw)
+    count_y, count_z = lax.axis_size("gy"), lax.axis_size("gz")
     periodic = count_y == 4
     if periodic:
-        lin = lax.all_gather(wide, "gy")
+        own = lax.all_gather(linear_field, "gy")
+        sides = []
+        for hops in (1, 2):
+            pairs = []
+            for y in range(count_y):
+                step = -hops if y % 2 == 0 else hops
+                pairs += [(y * count_z + (z + step) % count_z, y * count_z + z) for z in range(count_z)]
+            sides.append(lax.ppermute(own, ("gy", "gz"), pairs))
+        *sides, prepared = lax.optimization_barrier((*sides, prepared))
+        swap = [(y, y + 1 - 2 * (y % 2)) for y in range(count_y)]
+        fields = [own, *sides, *(lax.ppermute(side, "gy", swap) for side in sides)]
     else:
-        lin = jnp.stack([wide if h == 0 else lax.ppermute(wide, "gy", ring("gy", -h)) for h in range(-3, 4)])
+        send = functools.partial(lax.ppermute, axis_name="gz")
+        below = send(linear_field, perm=ring("gz", 1))
+        above = send(linear_field, perm=ring("gz", -1))
+        below_2 = send(linear_field[:, :, 4:], perm=ring("gz", 2))
+        above_2 = send(linear_field[:, :, :4], perm=ring("gz", -2))
+        wide = jnp.concatenate([below_2, below, linear_field, above, above_2], axis=2)
+        fields = [
+            jnp.stack([wide if h == 0 else lax.ppermute(wide, "gy", ring("gy", -h)) for h in range(-3, 4)])
+        ]
     me = lax.axis_index("gy").astype(jnp.int32).reshape(1)
 
-    lift_flat = lift_kernel.transpose(1, 0, 2).reshape(32, 81)
-    t_w, wf, wd1, wm, wd2, wmf = pl.pallas_call(
-        prep_kernel,
-        out_shape=[
-            jax.ShapeDtypeStruct(s, BF)
-            for s in ((256, 432), (96, 288), (64, 256), (192, 576), (128, 512), (96, 576))
-        ],
-        in_specs=[VMEM] * 7,
-        out_specs=[VMEM] * 6,
-        compiler_params=pltpu.CompilerParams(vmem_limit_bytes=16 << 20),
-    )(lift_flat, fine_kernel, reduce_first, middle_kernel, reduce_second, merge_fine, lift_spread().astype(BF))
+    t_w, wf, wf9, wd1, wm, wd2, wmf, split_f, split_ft, split_m, split_mt, taps = prepared
 
     r_lin, r_lift, r_fine, r_mid, r_skip, r_coarse = levels(periodic)
-    split_f, split_m = split_fine().astype(BF), split_middle().astype(BF)
-    head = jnp.pad(output_head, ((0, 13), (0, 0)))
     scratch = [
         pltpu.VMEM((r_lin.count, 4, 144, 128), BF),
-        pltpu.VMEM((r_lift.count, 30, 96, 128), BF),
+        pltpu.VMEM((r_lift.count, 30 * 96, 128), BF),
         pltpu.VMEM((r_fine.count, 28, 32, 128), BF),
         pltpu.VMEM((r_fine.count, 7, 128, 128), BF),
-        pltpu.VMEM((r_mid.count, 13 * 192, 128), BF),
         pltpu.VMEM((r_skip.count, 6, 64, 128), BF),
         pltpu.VMEM((r_skip.count, 256, 256), BF),
         pltpu.VMEM((r_coarse.count, 1152, 128), BF),
         pltpu.VMEM((6, 4, 64, 128), BF),
+        pltpu.VMEM((4, 3, 64, 128), BF),
         pltpu.VMEM((6, 7 * 384, 128), BF),
-        pltpu.VMEM((4, 3, 64, 128), BF),
-        pltpu.VMEM((6, 10, 192, 128), BF),
     ]
-    return pl.pallas_call(
-        functools.partial(net_kernel, periodic),
-        out_shape=jax.ShapeDtypeStruct(linear_field.shape, F32),
-        in_specs=[SMEM] + [VMEM] * 17,
-        out_specs=VMEM,
-        scratch_shapes=scratch,
-        compiler_params=pltpu.CompilerParams(vmem_limit_bytes=56 << 20),
-    )(
-        me,
-        lin,
+    weights = [
         t_w,
         wf,
+        wf9,
         wd1,
         wm,
         wd2,
@@ -430,13 +503,23 @@
         merge_middle,
         expand_first.reshape(256, 64),
         wmf,
-        head,
         split_f,
-        np.ascontiguousarray(split_f.T),
+        split_ft,
         split_m,
-        np.ascontiguousarray(split_m.T),
-        coarse_taps().astype(BF),
-    )
+        split_mt,
+        taps,
+    ]
+    scratch += [pltpu.VMEM(w.shape, BF) for w in weights]
+    scratch.append(pltpu.SemaphoreType.DMA((len(weights),)))
+    scratch += [pltpu.VMEM(f.shape, BF) for f in fields] + [pltpu.SemaphoreType.DMA((len(fields),))]
+    return pl.pallas_call(
+        functools.partial(net_kernel, periodic),
+        out_shape=jax.ShapeDtypeStruct(linear_field.shape, F32),
+        in_specs=[SMEM] + [ANY] * len(fields) + [VMEM] + [HBM] * len(weights),
+        out_specs=VMEM,
+        scratch_shapes=scratch,
+        compiler_params=pltpu.CompilerParams(vmem_limit_bytes=60 << 20),
+    )(me, *fields, output_head, *weights)
 
 
 def solution(mesh):

time: 66.3 us -> 53.8 us (0.81)
  local copies, waits for them, and re-layouts: 9.7 us -> 0.64 us
  starting transfers between devices: 9.9 us -> 4.28 us
  waiting for transfers between devices: 0.01 us -> 2.31 us
    unnamed x28 -> x10, local copies, waits for them, and re-layouts: 7.64 us -> 0.64 us
    ppermute x4, starting transfers between devices: 9.9 us -> 4.28 us  [the longest x2 3.51 us: body(): sides.append(lax.ppermute(own, ('gy', 'gz'), pairs))]
    pallas_call x1, Pallas kernels: 0.54 us -> 4.85 us  [body(): pl.pallas_call(prep_kernel, out_shape=[jax.ShapeDtypeStruct(s, BF) for s...]
    pallas_call x1, Pallas kernels: 38.7 us -> 34.9 us  [body(): pl.pallas_call(functools.partial(net_kernel, periodic), out_shape=jax.Sha...]
    ppermute x4, waiting for transfers between devices: 0.01 us -> 2.31 us  [the longest x2 1.22 us: body(): fields = [own, *sides, *(lax.ppermute(side, 'gy', swap) for side in sides)]]
    slice x1 -> x0, local copies, waits for them, and re-layouts: 0.82 us -> none  [body(): above_2 = send(linear_field[:, :, :4], perm=ring('gz', -2))]
  transfers between devices with their start and end apart: 4 -> 4, of which waited for: 0 -> 3; matrix products, arithmetic and copies ran while one was open for 5% -> 0% of each run, Pallas kernels for 1% -> 9%
where the time goes in v1:
time: 53.8 us; the launch traced here: 53.6 us
  Pallas kernels  39.8 us (74%)
  blocking collectives  6.53 us (12%)
  starting transfers between devices  4.28 us (8%)
  waiting for transfers between devices  2.31 us (4%)
  local copies, waits for them, and re-layouts  0.64 us (1%)
    pallas_call x1, Pallas kernels, body(): pl.pallas_call(functools.partial(net_kernel, periodic), out_shape=jax.Sha...  34.9 us
    all_gather x1, blocking collectives, body(): own = lax.all_gather(linear_field, 'gy')  6.53 us
    pallas_call x1, Pallas kernels, body(): pl.pallas_call(prep_kernel, out_shape=[jax.ShapeDtypeStruct(s, BF) for s...  4.85 us
    ppermute x2, starting transfers between devices, body(): sides.append(lax.ppermute(own, ('gy', 'gz'), pairs))  3.51 us
    ppermute x2, waiting for transfers between devices, body(): fields = [own, *sides, *(lax.ppermute(side, 'gy', swap) for side in sides)]  1.22 us
    ppermute x2, waiting for transfers between devices, body(): sides.append(lax.ppermute(own, ('gy', 'gz'), pairs))  1.09 us
  transfers between devices with their start and end apart: 4, of which 3 were waited for; matrix products, arithmetic and copies ran while one was open for 0% of the time, Pallas kernels for 9%

profile of v1, /device:TPU:0, one launch (start us, length us, event | category | flops | bytes accessed | tf_op | source)
XLA Modules:
  0.0 53.6 jit_solution(3768233990344448080)
XLA Ops:
  0.0 6.5 %all-gather = bf16[12,4,8,128]{3,2,1,0:T(8,128)(2,1)S(1)} all-gather(bf16[3,4,8,128]{3,2,1,0:T(8,128)(2,1)} %param.12), channel_id=2, replica_groups=mesh['gy'=4,'gz'=8] {'gy'}, dimensions={0}, use_global_device_ids=true | all-gather | bytes 122880 | tf_op jit(solution)/shard_map/all_gather | solution.py:456
  6.5 0.0 copy-start
  6.5 2.0 %collective-permute-start.1 = (bf16[4,3,4,8,128]{4,3,2,1,0:T(8,128)(2,1)S(1)}, bf16[4,3,4,8,128]{4,3,2,1,0:T(8,128)(2,1)S(1)}, u32[]{:S(2)}, u32[]{:S(2)}) collective-permute-start(bf16[4,3,4,8,128]{4,3,2,1,0:T(8,128)(2,1)S(1)} %bitcast.11), channel_id=1, source_target_pairs={{6,0},{7,1},{0,2},{1,3},{2,4},{3,5},{4,6},{5,7},{10,8},{11,9},{12,... | collective-permute-start | bytes 294920 | tf_op jit(solution)/shard_map/ppermute | solution.py:463
  8.6 1.5 %collective-permute-start = (bf16[4,3,4,8,128]{4,3,2,1,0:T(8,128)(2,1)S(1)}, bf16[4,3,4,8,128]{4,3,2,1,0:T(8,128)(2,1)S(1)}, u32[]{:S(2)}, u32[]{:S(2)}) collective-permute-start(bf16[4,3,4,8,128]{4,3,2,1,0:T(8,128)(2,1)S(1)} %bitcast.12), channel_id=1, source_target_pairs={{7,0},{0,1},{1,2},{2,3},{3,4},{4,5},{5,6},{6,7},{9,8},{10,9},{11,1... | collective-permute-start | bytes 294920 | tf_op jit(solution)/shard_map/ppermute | solution.py:463
  10.1 4.9 %shard_map.118 = (bf16[256,432]{1,0:T(8,128)(2,1)}, bf16[96,256]{1,0:T(8,128)(2,1)}, bf16[32,96]{1,0:T(8,128)(2,1)}, bf16[64,256]{1,0:T(8,128)(2,1)}, bf16[192,5...) custom-call(bf16[3,27,32]{2,1,0:T(8,128)(2,1)} %bitcast.18, ...), custom_call_target="tpu_custom_call" | custom-call | flops 4000000000 | bytes 10000000 | tf_op jit(solution)/shard_map/pallas_call | solution.py:442
  14.9 0.0 copy-done
  14.9 0.0 collective-permute-done.1.refs_2_
  14.9 0.0 copy-start.1
  14.9 1.1 %collective-permute-done.refs_1_ = bf16[4,3,4,8,128]{4,3,2,1,0:T(8,128)(2,1)S(1)} collective-permute-done((bf16[4,3,4,8,128]{4,3,2,1,0:T(8,128)(2,1)S(1)}, bf16[4,3,4,8,128]{4,3,2,1,0:T(8,128)(2,1)S(1)}, u32[]{:S(2)}, u32[]{:S(2)}) %collective-permute-start) | collective-permute-done | bytes 98336 | tf_op jit(solution)/shard_map/ppermute | solution.py:463
  16.0 0.0 copy-start.2
  16.0 0.7 %collective-permute-start.2 = (bf16[4,3,4,8,128]{4,3,2,1,0:T(8,128)(2,1)S(1)}, bf16[4,3,4,8,128]{4,3,2,1,0:T(8,128)(2,1)S(1)}, u32[]{:S(2)}, u32[]{:S(2)}) collective-permute-start(bf16[4,3,4,8,128]{4,3,2,1,0:T(8,128)(2,1)S(1)} %collective-permute-done.refs_1_), channel_id=1, source_target_pairs={{0,8},{8,0},{16,24},{24,16},{1,9},{9,1},{17,25},{25,17},{2,10},{10... | collective-permute-start | bytes 294920 | tf_op jit(solution)/shard_map/ppermute | solution.py:466
  16.7 0.1 collective-permute-start.3
  16.8 0.9 %collective-permute-done.2.refs_3_ = bf16[4,3,4,8,128]{4,3,2,1,0:T(8,128)(2,1)S(1)} collective-permute-done((bf16[4,3,4,8,128]{4,3,2,1,0:T(8,128)(2,1)S(1)}, bf16[4,3,4,8,128]{4,3,2,1,0:T(8,128)(2,1)S(1)}, u32[]{:S(2)}, u32[]{:S(2)}) %collective-permute-start.2) | collective-permute-done | bytes 98336 | tf_op jit(solution)/shard_map/ppermute | solution.py:466
  17.7 0.0 copy-start.3
  17.7 0.4 collective-permute-done.3.refs_4_
  18.0 0.0 copy-start.4
  18.0 0.0 copy-done.1
  18.0 0.0 copy-done.2
  18.0 0.3 copy-done.3
  18.3 0.3 copy-done.4
  18.7 34.9 %shard_map.119 = f32[3,4,8,128]{3,2,1,0:T(8,128)} custom-call(s32[1]{0:T(128)} %bitcast.me, bf16[4,3,4,8,128]{4,3,2,1,0:T(8,128)(2,1)} %bitcast.13, bf16[4,3,4,8,128]{4,3,2,1,0:T(8,128)(2,1)} %copy-done.2, bf16[4,3,4,8,128]{4,3,2,1,0:T(8,128)(2,1)} %copy-done.1, bf16[4,3,4,8,128]{4,3,2,1,0:T(8,128)(2,1)} %copy-done.3, bf16[4,3,4,8,128]{4,3,2,1,0:T(8,128)(2,1)} %copy-done.4, ...), custom_call_target="tpu_custom_call" | custom-call | tf_op jit(solution)/shard_map/pallas_call | solution.py:515
Async XLA Ops:
  6.5 8.4 %copy-start = (bf16[12,4,8,128]{3,2,1,0:T(8,128)(2,1)}, bf16[12,4,8,128]{3,2,1,0:T(8,128)(2,1)S(1)}, u32[]{:S(2)}) copy-start(bf16[12,4,8,128]{3,2,1,0:T(8,128)(2,1)S(1)} %all-gather) | copy-start | bytes 294916
  6.5 8.4 %collective-permute-start.1 = (bf16[4,3,4,8,128]{4,3,2,1,0:T(8,128)(2,1)S(1)}, bf16[4,3,4,8,128]{4,3,2,1,0:T(8,128)(2,1)S(1)}, u32[]{:S(2)}, u32[]{:S(2)}) collective-permute-start(bf16[4,3,4,8,128]{4,3,2,1,0:T(8,128)(2,1)S(1)} %bitcast.11), channel_id=1, source_target_pairs={{6,0},{7,1},{0,2},{1,3},{2,4},{3,5},{4,6},{5,7},{10,8},{11,9},{12,... | collective-permute-start | bytes 294920 | tf_op jit(solution)/shard_map/ppermute | solution.py:463
  8.6 7.5 %collective-permute-start = (bf16[4,3,4,8,128]{4,3,2,1,0:T(8,128)(2,1)S(1)}, bf16[4,3,4,8,128]{4,3,2,1,0:T(8,128)(2,1)S(1)}, u32[]{:S(2)}, u32[]{:S(2)}) collective-permute-start(bf16[4,3,4,8,128]{4,3,2,1,0:T(8,128)(2,1)S(1)} %bitcast.12), channel_id=1, source_target_pairs={{7,0},{0,1},{1,2},{2,3},{3,4},{4,5},{5,6},{6,7},{9,8},{10,9},{11,1... | collective-permute-start | bytes 294920 | tf_op jit(solution)/shard_map/ppermute | solution.py:463
  14.9 3.1 %copy-start.1 = (bf16[4,3,4,8,128]{4,3,2,1,0:T(8,128)(2,1)}, bf16[4,3,4,8,128]{4,3,2,1,0:T(8,128)(2,1)S(1)}, u32[]{:S(2)}) copy-start(bf16[4,3,4,8,128]{4,3,2,1,0:T(8,128)(2,1)S(1)} %collective-permute-done.1.refs_2_) | copy-start | bytes 294916
  16.0 2.0 %copy-start.2 = (bf16[4,3,4,8,128]{4,3,2,1,0:T(8,128)(2,1)}, bf16[4,3,4,8,128]{4,3,2,1,0:T(8,128)(2,1)S(1)}, u32[]{:S(2)}) copy-start(bf16[4,3,4,8,128]{4,3,2,1,0:T(8,128)(2,1)S(1)} %collective-permute-done.refs_1_) | copy-start | bytes 294916
  16.0 1.6 %collective-permute-start.2 = (bf16[4,3,4,8,128]{4,3,2,1,0:T(8,128)(2,1)S(1)}, bf16[4,3,4,8,128]{4,3,2,1,0:T(8,128)(2,1)S(1)}, u32[]{:S(2)}, u32[]{:S(2)}) collective-permute-start(bf16[4,3,4,8,128]{4,3,2,1,0:T(8,128)(2,1)S(1)} %collective-permute-done.refs_1_), channel_id=1, source_target_pairs={{0,8},{8,0},{16,24},{24,16},{1,9},{9,1},{17,25},{25,17},{2,10},{10... | collective-permute-start | bytes 294920 | tf_op jit(solution)/shard_map/ppermute | solution.py:466
  16.7 1.3 %collective-permute-start.3 = (bf16[4,3,4,8,128]{4,3,2,1,0:T(8,128)(2,1)S(1)}, bf16[4,3,4,8,128]{4,3,2,1,0:T(8,128)(2,1)S(1)}, u32[]{:S(2)}, u32[]{:S(2)}) collective-permute-start(bf16[4,3,4,8,128]{4,3,2,1,0:T(8,128)(2,1)S(1)} %collective-permute-done.1.refs_2_), channel_id=1, source_target_pairs={{0,8},{8,0},{16,24},{24,16},{1,9},{9,1},{17,25},{25,17},{2,10},{10... | collective-permute-start | bytes 294920 | tf_op jit(solution)/shard_map/ppermute | solution.py:466
  17.7 0.6 %copy-start.3 = (bf16[4,3,4,8,128]{4,3,2,1,0:T(8,128)(2,1)}, bf16[4,3,4,8,128]{4,3,2,1,0:T(8,128)(2,1)S(1)}, u32[]{:S(2)}) copy-start(bf16[4,3,4,8,128]{4,3,2,1,0:T(8,128)(2,1)S(1)} %collective-permute-done.2.refs_3_) | copy-start | bytes 294916
  18.0 0.6 %copy-start.4 = (bf16[4,3,4,8,128]{4,3,2,1,0:T(8,128)(2,1)}, bf16[4,3,4,8,128]{4,3,2,1,0:T(8,128)(2,1)S(1)}, u32[]{:S(2)}) copy-start(bf16[4,3,4,8,128]{4,3,2,1,0:T(8,128)(2,1)S(1)} %collective-permute-done.3.refs_4_) | copy-start | bytes 294916

commit v2 on v1

--- a/solution.py
+++ b/solution.py
@@ -54,8 +54,8 @@
 
 def prep_kernel(lift, *refs):
     sources, refs = refs[:5], refs[5:]
-    results, refs = refs[:12], refs[12:]
-    (t_o, wf_o, wf9_o, wd1_o, wm_o, wd2_o, wmf_o, sf_o, sft_o, sm_o, smt_o, st_o), refs = refs[:12], refs[12:]
+    results, refs = refs[:13], refs[13:]
+    (t_o, wf_o, wf9_o, wd1_o, wm_o, wm9_o, wd2_o, wmf_o, sf_o, sft_o, sm_o, smt_o, st_o), refs = refs[:13], refs[13:]
     (fine, red1, mid, red2, mfine), sems, out_sems = refs[:5], refs[5], refs[6]
     copies = [pltpu.make_async_copy(src, dst, sems.at[i]) for i, (src, dst) in enumerate(zip(sources, refs))]
     for copy in copies:
@@ -77,6 +77,7 @@
         t_o[32 * zo : 32 * zo + 32] = moved[:, :432].astype(BF)
     for copy in copies:
         copy.wait()
+    wf9_o[...] = jnp.zeros_like(wf9_o)
     for dz in range(3):
         for dy in range(3):
             for dx in range(3):
@@ -84,13 +85,17 @@
                 if k < 8:
                     wf_o[32 * dz : 32 * dz + 32, 32 * k : 32 * k + 32] = fine[9 * dy + 3 * dz + dx]
                 else:
-                    wf9_o[:, 32 * dz : 32 * dz + 32] = fine[9 * dy + 3 * dz + dx]
+                    for zo in range(2):
+                        wf9_o[32 * zo : 32 * zo + 32, 32 * (dz + zo) : 32 * (dz + zo) + 32] = fine[9 * dy + 3 * dz + dx]
                 wmf_o[32 * dz : 32 * dz + 32, 64 * k : 64 * k + 64] = mfine[9 * dy + 3 * dz + dx]
                 j = 3 * dz + dx
-                wm_o[64 * dy : 64 * dy + 64, 64 * j : 64 * j + 64] = mid[9 * dy + 3 * dz + dx]
+                if j < 8:
+                    wm_o[64 * dy : 64 * dy + 64, 64 * j : 64 * j + 64] = mid[9 * dy + 3 * dz + dx]
+                else:
+                    wm9_o[:, 64 * dy : 64 * dy + 64] = mid[9 * dy + 3 * dz + dx]
     wd1_o[...] = red1[...].astype(F32).T.astype(BF)
     wd2_o[...] = red2[...].astype(F32).T.astype(BF)
-    made = (t_o, wf_o, wf9_o, wd1_o, wm_o, wd2_o, wmf_o, sf_o, sft_o, sm_o, smt_o, st_o)
+    made = (t_o, wf_o, wf9_o, wd1_o, wm_o, wm9_o, wd2_o, wmf_o, sf_o, sft_o, sm_o, smt_o, st_o)
     copies = [pltpu.make_async_copy(src, dst, out_sems.at[i]) for i, (src, dst) in enumerate(zip(made, results))]
     for copy in copies:
         copy.start()
@@ -123,34 +128,45 @@
     )
 
 
-def shifted_64(v, lane):
-    edge_low = (lane & 63) == 0
-    edge_high = (lane & 63) == 63
-    low = jnp.where(edge_low, pltpu.roll(v, 65, 1), pltpu.roll(v, 1, 1))
-    high = jnp.where(edge_high, pltpu.roll(v, 63, 1), pltpu.roll(v, 127, 1))
-    return low, high
+def shifted_rows(direct):
+    lane = lax.broadcasted_iota(jnp.int32, direct[0].shape, 1)
+    first = lane < 64
+    edges = (lane & 63) == 0, (lane & 63) == 63
+    kept, swapped = [], []
+    for v in direct:
+        t = pltpu.roll(v, 64, 1)
+        pairs = [(pltpu.roll(v, n, 1), pltpu.roll(t, n, 1)) for n in (1, 127)]
+        low, high = (jnp.where(edge, rt, rv) for edge, (rv, rt) in zip(edges, pairs))
+        low_t, high_t = (jnp.where(edge, rv, rt) for edge, (rv, rt) in zip(edges, pairs))
+        kept.append((low, v, high))
+        swapped.append((low_t, t, high_t))
+    result = []
+    for p in range(len(direct)):
+        result.append(kept[p])
+        if p + 1 < len(direct):
+            result.append(tuple(jnp.where(first, u, w) for u, w in zip(swapped[p], swapped[p + 1])))
+    return result
 
 
 def net_kernel(periodic, me, *refs):
     count = 5 if periodic else 1
     fields, refs = refs[:count], refs[count:]
-    head, weights, out, refs = refs[0], refs[1:17], refs[17], refs[18:]
+    head, weights, out, refs = refs[0], refs[1:18], refs[18], refs[19:]
     pat, lifted, fine, halves, mskip, quarters, ctaps, ups, mout, joined = refs[:10]
-    held, sems = refs[10:26], refs[26]
-    near_by, field_sems = refs[27 : 27 + count], refs[27 + count]
+    held, sems = refs[10:27], refs[27]
+    near_by, field_sems = refs[28 : 28 + count], refs[28 + count]
     field_copies = [
         pltpu.make_async_copy(src, dst, field_sems.at[i]) for i, (src, dst) in enumerate(zip(fields, near_by))
     ]
     for copy in field_copies:
         copy.start()
+    copies = [pltpu.make_async_copy(src, dst, sems.at[i]) for i, (src, dst) in enumerate(zip(weights, held))]
+    copies[0].start()
     if periodic:
         own, near, far, other_near, other_far = near_by
     else:
         wide = near_by[0]
-    copies = [pltpu.make_async_copy(src, dst, sems.at[i]) for i, (src, dst) in enumerate(zip(weights, held))]
-    for copy in copies:
-        copy.start()
-    (t_w, wf, wf9, wd1, wm, wd2, ck, we2, mmk, we1, wmf, s_fine, s_fine_t, s_mid, s_mid_t, s_taps) = held
+    (t_w, wf, wf9, s_fine, wd1, wm, wm9, s_mid, wd2, s_taps, ck, we2, s_mid_t, mmk, we1, s_fine_t, wmf) = held
 
     def need(*names):
         for name in names:
@@ -182,7 +198,9 @@
                     pat[k, j, (3 * c + dx) * 16 : (3 * c + dx) * 16 + 16] = v[8 * j : 8 * j + 16].astype(BF)
         return carry
 
-    lax.fori_loop(0, r_lin.count, patch, 0)
+    lax.fori_loop(0, r_lin.count, patch, 0, unroll=8)
+    for copy in copies[1:]:
+        copy.start()
 
     need(t_w)
 
@@ -202,7 +220,7 @@
                         lifted[k, 96 * z + 64 : 96 * z + 96] = pltpu.roll(v, 127, 1).astype(BF)
         return carry
 
-    lax.fori_loop(0, r_lift.count, lift, 0, unroll=2)
+    lax.fori_loop(0, r_lift.count, lift, 0, unroll=8)
 
     need(wf, wf9, s_fine)
 
@@ -218,14 +236,14 @@
             r = dot(wf[...], jnp.concatenate(cols, axis=1))
             parts += [r[:, :128], r[:, 128:]]
         rows = []
-        for pair in range(14):
-            last = [lifted[ys[2], 96 * (2 * pair + i) + 64 : 96 * (2 * pair + i) + 96] for i in range(4)]
-            cols = [jnp.concatenate(last[h : h + 3], axis=0) for h in range(2)]
+        last = [lifted[ys[2], 96 * z + 64 : 96 * z + 96] for z in range(30)]
+        for quad in range(7):
+            cols = [jnp.concatenate(last[4 * quad + 2 * h : 4 * quad + 2 * h + 4], axis=0) for h in range(2)]
             r = dot(wf9[...], jnp.concatenate(cols, axis=1))
-            for h in range(2):
-                z = 2 * pair + h
-                v = parts[z][0:32] + parts[z + 1][32:64] + parts[z + 2][64:96] + r[:, 128 * h : 128 * h + 128]
-                v = act(v).astype(BF)
+            for i in range(4):
+                z, zo, h = 4 * quad + i, i % 2, i // 2
+                v = parts[z][0:32] + parts[z + 1][32:64] + parts[z + 2][64:96]
+                v = act(v + r[32 * zo : 32 * zo + 32, 128 * h : 128 * h + 128]).astype(BF)
                 fine[k, z] = v
                 rows.append(v)
         left = []
@@ -240,9 +258,7 @@
                 ]
         return carry
 
-    lax.fori_loop(0, r_fine.count, fine_conv, 0, unroll=2)
-
-    lane = lax.broadcasted_iota(jnp.int32, (64, 128), 1)
+    lax.fori_loop(0, r_fine.count, fine_conv, 0, unroll=8)
 
     need(wd1)
 
@@ -257,34 +273,34 @@
             for h in range(2):
                 direct[h].append(r[:, 128 * h : 128 * h + 128])
         for h in range(2):
-            turned = [pltpu.roll(v, 64, 1) for v in direct[h]]
-            for pos in range(13):
-                p = pos // 2
-                v = direct[h][p] if pos % 2 == 0 else jnp.where(lane < 64, turned[p], turned[p + 1])
-                low, high = shifted_64(v, lane)
-                for dx, u in enumerate((low, v, high)):
+            for pos, triple in enumerate(shifted_rows(direct[h])):
+                for dx, u in enumerate(triple):
                     at = pos * 192 + dx * 64
                     lifted[2 * k + h, at : at + 64] = u.astype(BF)
         return carry
 
     lax.fori_loop(0, r_mid.count // 2, middle_in, 0)
 
-    need(wm)
+    need(wm, wm9)
 
     def middle_conv(k, carry):
         parts = []
         start = pl.multiple_of(k * 384, 384)
         for pair in range(r_mid.count // 2):
-            cols = [lifted[2 * pair + h, pl.ds(start, 576)] for h in range(2)]
+            cols = [lifted[2 * pair + h, pl.ds(start, 512)] for h in range(2)]
             r = dot(wm[...], jnp.concatenate(cols, axis=1))
             parts += [r[:, :128], r[:, 128:]]
-        for y in range(r_skip.count):
-            rel = y + r_skip.low
-            v = sum(parts[r_mid.at(rel + dy - 1)][64 * dy : 64 * dy + 64] for dy in range(3))
-            mskip[y, k] = act(v).astype(BF)
+        last = [lifted[y, pl.ds(start + 512, 64)] for y in range(r_mid.count)]
+        for pair in range(r_skip.count // 2):
+            rels = [2 * pair + h + r_skip.low for h in range(2)]
+            cols = [jnp.concatenate([last[r_mid.at(rel + dy)] for dy in (-1, 0, 1)], axis=0) for rel in rels]
+            r = dot(wm9[...], jnp.concatenate(cols, axis=1))
+            for h, rel in enumerate(rels):
+                v = sum(parts[r_mid.at(rel + dy - 1)][64 * dy : 64 * dy + 64] for dy in range(3))
+                mskip[2 * pair + h, k] = act(v + r[:, 128 * h : 128 * h + 128]).astype(BF)
         return carry
 
-    lax.fori_loop(0, 6, middle_conv, 0)
+    lax.fori_loop(0, 6, middle_conv, 0, unroll=True)
 
     need(s_mid, wd2, s_taps)
 
@@ -299,13 +315,15 @@
                 quarters[y, t * 64 : t * 64 + 64, 128 * chunk : 128 * chunk + 128] = s[
                     64 * y : 64 * y + 64, 128 * t : 128 * t + 128
                 ]
+    cin = []
     for y in range(r_coarse.count):
         rel = 2 * (y + r_coarse.low)
         right = jnp.concatenate([quarters[r_skip.at(rel + a)] for a in range(2)], axis=0)
-        cin = act(dot(wd2[...], right)).astype(BF)
-        taps = dot(cin, s_taps[...]).astype(BF)
+        cin.append(act(dot(wd2[...], right)).astype(BF))
+    taps = dot(jnp.concatenate(cin, axis=0), s_taps[...]).astype(BF)
+    for y in range(r_coarse.count):
         for t in range(9):
-            ctaps[y, 128 * t : 128 * t + 128] = taps[:, 128 * t : 128 * t + 128]
+            ctaps[y, 128 * t : 128 * t + 128] = taps[128 * y : 128 * y + 128, 128 * t : 128 * t + 128]
 
     need(ck, we2, s_mid_t)
 
@@ -315,28 +333,24 @@
         cols = [jnp.concatenate([ctaps[r_coarse.at(rel + dy)] for dy in (-1, 0, 1)], axis=0) for rel in rels]
         cout = act(dot(wc, jnp.concatenate(cols, axis=1))).astype(BF)
         u = act(dot(we2[...], cout)).astype(BF)
+        rows = []
         for h in range(2 if first < 1 else 1):
             for a in range(2):
-                left = jnp.concatenate(
-                    [u[(4 * a + t) * 64 : (4 * a + t) * 64 + 64, 128 * h : 128 * h + 128] for t in range(4)], axis=1
-                )
-                s = dot(left, s_mid_t[...]).astype(BF)
-                for q in range(4):
-                    ups[2 * (first + 1 + h) + a, q] = s[:, 128 * q : 128 * q + 128]
+                blocks = [u[(4 * a + t) * 64 : (4 * a + t) * 64 + 64, 128 * h : 128 * h + 128] for t in range(4)]
+                rows.append(jnp.concatenate(blocks, axis=1))
+        s = dot(jnp.concatenate(rows, axis=0), s_mid_t[...]).astype(BF)
+        for i in range(len(rows)):
+            for q in range(4):
+                ups[2 * (first + 1) + i, q] = s[64 * i : 64 * i + 64, 128 * q : 128 * q + 128]
 
     need(mmk)
 
-    lane128 = lax.broadcasted_iota(jnp.int32, (128, 128), 1)
     for y in range(6):
         direct = [
             jnp.concatenate([ups[y, q], mskip[r_skip.at(y - 2), q + 1]], axis=0).astype(F32) for q in range(4)
         ]
-        turned = [pltpu.roll(v, 64, 1) for v in direct]
-        for pos in range(7):
-            p = pos // 2
-            v = direct[p] if pos % 2 == 0 else jnp.where(lane128 < 64, turned[p], turned[p + 1])
-            low, high = shifted_64(v, lane128)
-            for dx, u in enumerate((low, v, high)):
+        for pos, triple in enumerate(shifted_rows(direct)):
+            for dx, u in enumerate(triple):
                 at = pos * 384 + dx * 128
                 joined[y, at : at + 128] = u.astype(BF)
     wmm = jnp.concatenate(
@@ -428,9 +442,10 @@
     forms = [
         (256, 432),
         (96, 256),
-        (32, 96),
+        (64, 128),
         (64, 256),
-        (192, 576),
+        (192, 512),
+        (64, 192),
         (128, 512),
         (96, 576),
         (256, 256),
@@ -476,7 +491,7 @@
         ]
     me = lax.axis_index("gy").astype(jnp.int32).reshape(1)
 
-    t_w, wf, wf9, wd1, wm, wd2, wmf, split_f, split_ft, split_m, split_mt, taps = prepared
+    t_w, wf, wf9, wd1, wm, wm9, wd2, wmf, split_f, split_ft, split_m, split_mt, taps = prepared
 
     r_lin, r_lift, r_fine, r_mid, r_skip, r_coarse = levels(periodic)
     scratch = [
@@ -495,19 +510,20 @@
         t_w,
         wf,
         wf9,
+        split_f,
         wd1,
         wm,
+        wm9,
+        split_m,
         wd2,
+        taps,
         coarse_kernel,
         expand_second.reshape(512, 128),
+        split_mt,
         merge_middle,
         expand_first.reshape(256, 64),
+        split_ft,
         wmf,
-        split_f,
-        split_ft,
-        split_m,
-        split_mt,
-        taps,
     ]
     scratch += [pltpu.VMEM(w.shape, BF) for w in weights]
     scratch.append(pltpu.SemaphoreType.DMA((len(weights),)))

time: 53.8 us -> 45.2 us (0.84)
  Pallas kernels: 39.8 us -> 31 us
    pallas_call x1, Pallas kernels: 34.9 us -> 26.1 us  [body(): pl.pallas_call(functools.partial(net_kernel, periodic), out_shape=jax.Sha...]
  transfers between devices with their start and end apart: 4 -> 4, of which waited for: 3 -> 3; matrix products, arithmetic and copies ran while one was open for 0% -> 0% of each run, Pallas kernels for 9% -> 11%
where the time goes in v2:
time: 45.2 us; the launch traced here: 45 us
  Pallas kernels  31 us (69%)
  blocking collectives  6.53 us (14%)
  starting transfers between devices  4.33 us (10%)
  waiting for transfers between devices  2.26 us (5%)
  local copies, waits for them, and re-layouts  0.64 us (1%)
    pallas_call x1, Pallas kernels, body(): pl.pallas_call(functools.partial(net_kernel, periodic), out_shape=jax.Sha...  26.1 us
    all_gather x1, blocking collectives, body(): own = lax.all_gather(linear_field, 'gy')  6.53 us
    pallas_call x1, Pallas kernels, body(): pl.pallas_call(prep_kernel, out_shape=[jax.ShapeDtypeStruct(s, BF) for s...  4.9 us
    ppermute x2, starting transfers between devices, body(): sides.append(lax.ppermute(own, ('gy', 'gz'), pairs))  3.51 us
    ppermute x2, waiting for transfers between devices, body(): fields = [own, *sides, *(lax.ppermute(side, 'gy', swap) for side in sides)]  1.22 us
    ppermute x2, waiting for transfers between devices, body(): sides.append(lax.ppermute(own, ('gy', 'gz'), pairs))  1.04 us
  transfers between devices with their start and end apart: 4, of which 3 were waited for; matrix products, arithmetic and copies ran while one was open for 0% of the time, Pallas kernels for 11%

profile of v2, /device:TPU:0, one launch (start us, length us, event | category | flops | bytes accessed | tf_op | source)
XLA Modules:
  0.0 45.0 jit_solution(16415145390437361859)
XLA Ops:
  0.0 6.5 %all-gather = bf16[12,4,8,128]{3,2,1,0:T(8,128)(2,1)S(1)} all-gather(bf16[3,4,8,128]{3,2,1,0:T(8,128)(2,1)} %param.12), channel_id=2, replica_groups=mesh['gy'=4,'gz'=8] {'gy'}, dimensions={0}, use_global_device_ids=true | all-gather | bytes 122880 | tf_op jit(solution)/shard_map/all_gather | solution.py:471
  6.5 0.0 copy-start
  6.5 2.0 %collective-permute-start.1 = (bf16[4,3,4,8,128]{4,3,2,1,0:T(8,128)(2,1)S(1)}, bf16[4,3,4,8,128]{4,3,2,1,0:T(8,128)(2,1)S(1)}, u32[]{:S(2)}, u32[]{:S(2)}) collective-permute-start(bf16[4,3,4,8,128]{4,3,2,1,0:T(8,128)(2,1)S(1)} %bitcast.11), channel_id=1, source_target_pairs={{6,0},{7,1},{0,2},{1,3},{2,4},{3,5},{4,6},{5,7},{10,8},{11,9},{12,... | collective-permute-start | bytes 294920 | tf_op jit(solution)/shard_map/ppermute | solution.py:478
  8.6 1.5 %collective-permute-start = (bf16[4,3,4,8,128]{4,3,2,1,0:T(8,128)(2,1)S(1)}, bf16[4,3,4,8,128]{4,3,2,1,0:T(8,128)(2,1)S(1)}, u32[]{:S(2)}, u32[]{:S(2)}) collective-permute-start(bf16[4,3,4,8,128]{4,3,2,1,0:T(8,128)(2,1)S(1)} %bitcast.12), channel_id=1, source_target_pairs={{7,0},{0,1},{1,2},{2,3},{3,4},{4,5},{5,6},{6,7},{9,8},{10,9},{11,1... | collective-permute-start | bytes 294920 | tf_op jit(solution)/shard_map/ppermute | solution.py:478
  10.1 4.9 %shard_map.118 = (bf16[256,432]{1,0:T(8,128)(2,1)}, bf16[96,256]{1,0:T(8,128)(2,1)}, bf16[64,128]{1,0:T(8,128)(2,1)}, bf16[64,256]{1,0:T(8,128)(2,1)}, bf16[192,...) custom-call(bf16[3,27,32]{2,1,0:T(8,128)(2,1)} %bitcast.18, ...), custom_call_target="tpu_custom_call" | custom-call | flops 4000000000 | bytes 10000000 | tf_op jit(solution)/shard_map/pallas_call | solution.py:457
  15.0 0.0 copy-done
  15.0 0.0 collective-permute-done.1.refs_2_
  15.0 0.0 copy-start.1
  15.0 1.0 %collective-permute-done.refs_1_ = bf16[4,3,4,8,128]{4,3,2,1,0:T(8,128)(2,1)S(1)} collective-permute-done((bf16[4,3,4,8,128]{4,3,2,1,0:T(8,128)(2,1)S(1)}, bf16[4,3,4,8,128]{4,3,2,1,0:T(8,128)(2,1)S(1)}, u32[]{:S(2)}, u32[]{:S(2)}) %collective-permute-start) | collective-permute-done | bytes 98336 | tf_op jit(solution)/shard_map/ppermute | solution.py:478
  16.0 0.0 copy-start.2
  16.0 0.7 %collective-permute-start.2 = (bf16[4,3,4,8,128]{4,3,2,1,0:T(8,128)(2,1)S(1)}, bf16[4,3,4,8,128]{4,3,2,1,0:T(8,128)(2,1)S(1)}, u32[]{:S(2)}, u32[]{:S(2)}) collective-permute-start(bf16[4,3,4,8,128]{4,3,2,1,0:T(8,128)(2,1)S(1)} %collective-permute-done.refs_1_), channel_id=1, source_target_pairs={{0,8},{8,0},{16,24},{24,16},{1,9},{9,1},{17,25},{25,17},{2,10},{10... | collective-permute-start | bytes 294920 | tf_op jit(solution)/shard_map/ppermute | solution.py:481
  16.8 0.1 collective-permute-start.3
  16.9 0.9 %collective-permute-done.2.refs_3_ = bf16[4,3,4,8,128]{4,3,2,1,0:T(8,128)(2,1)S(1)} collective-permute-done((bf16[4,3,4,8,128]{4,3,2,1,0:T(8,128)(2,1)S(1)}, bf16[4,3,4,8,128]{4,3,2,1,0:T(8,128)(2,1)S(1)}, u32[]{:S(2)}, u32[]{:S(2)}) %collective-permute-start.2) | collective-permute-done | bytes 98336 | tf_op jit(solution)/shard_map/ppermute | solution.py:481
  17.7 0.0 copy-start.3
  17.7 0.4 collective-permute-done.3.refs_4_
  18.1 0.0 copy-start.4
  18.1 0.0 copy-done.1
  18.1 0.0 copy-done.2
  18.1 0.3 copy-done.3
  18.4 0.4 copy-done.4
  18.7 26.1 %shard_map.119 = f32[3,4,8,128]{3,2,1,0:T(8,128)} custom-call(s32[1]{0:T(128)} %bitcast.me, bf16[4,3,4,8,128]{4,3,2,1,0:T(8,128)(2,1)} %bitcast.13, bf16[4,3,4,8,128]{4,3,2,1,0:T(8,128)(2,1)} %copy-done.2, bf16[4,3,4,8,128]{4,3,2,1,0:T(8,128)(2,1)} %copy-done.1, bf16[4,3,4,8,128]{4,3,2,1,0:T(8,128)(2,1)} %copy-done.3, bf16[4,3,4,8,128]{4,3,2,1,0:T(8,128)(2,1)} %copy-done.4, ...), custom_call_target="tpu_custom_call" | custom-call | tf_op jit(solution)/shard_map/pallas_call | solution.py:531
Async XLA Ops:
  6.5 8.4 %copy-start = (bf16[12,4,8,128]{3,2,1,0:T(8,128)(2,1)}, bf16[12,4,8,128]{3,2,1,0:T(8,128)(2,1)S(1)}, u32[]{:S(2)}) copy-start(bf16[12,4,8,128]{3,2,1,0:T(8,128)(2,1)S(1)} %all-gather) | copy-start | bytes 294916
  6.5 8.4 %collective-permute-start.1 = (bf16[4,3,4,8,128]{4,3,2,1,0:T(8,128)(2,1)S(1)}, bf16[4,3,4,8,128]{4,3,2,1,0:T(8,128)(2,1)S(1)}, u32[]{:S(2)}, u32[]{:S(2)}) collective-permute-start(bf16[4,3,4,8,128]{4,3,2,1,0:T(8,128)(2,1)S(1)} %bitcast.11), channel_id=1, source_target_pairs={{6,0},{7,1},{0,2},{1,3},{2,4},{3,5},{4,6},{5,7},{10,8},{11,9},{12,... | collective-permute-start | bytes 294920 | tf_op jit(solution)/shard_map/ppermute | solution.py:478
  8.6 7.5 %collective-permute-start = (bf16[4,3,4,8,128]{4,3,2,1,0:T(8,128)(2,1)S(1)}, bf16[4,3,4,8,128]{4,3,2,1,0:T(8,128)(2,1)S(1)}, u32[]{:S(2)}, u32[]{:S(2)}) collective-permute-start(bf16[4,3,4,8,128]{4,3,2,1,0:T(8,128)(2,1)S(1)} %bitcast.12), channel_id=1, source_target_pairs={{7,0},{0,1},{1,2},{2,3},{3,4},{4,5},{5,6},{6,7},{9,8},{10,9},{11,1... | collective-permute-start | bytes 294920 | tf_op jit(solution)/shard_map/ppermute | solution.py:478
  15.0 3.1 %copy-start.1 = (bf16[4,3,4,8,128]{4,3,2,1,0:T(8,128)(2,1)}, bf16[4,3,4,8,128]{4,3,2,1,0:T(8,128)(2,1)S(1)}, u32[]{:S(2)}) copy-start(bf16[4,3,4,8,128]{4,3,2,1,0:T(8,128)(2,1)S(1)} %collective-permute-done.1.refs_2_) | copy-start | bytes 294916
  16.0 2.1 %copy-start.2 = (bf16[4,3,4,8,128]{4,3,2,1,0:T(8,128)(2,1)}, bf16[4,3,4,8,128]{4,3,2,1,0:T(8,128)(2,1)S(1)}, u32[]{:S(2)}) copy-start(bf16[4,3,4,8,128]{4,3,2,1,0:T(8,128)(2,1)S(1)} %collective-permute-done.refs_1_) | copy-start | bytes 294916
  16.0 1.7 %collective-permute-start.2 = (bf16[4,3,4,8,128]{4,3,2,1,0:T(8,128)(2,1)S(1)}, bf16[4,3,4,8,128]{4,3,2,1,0:T(8,128)(2,1)S(1)}, u32[]{:S(2)}, u32[]{:S(2)}) collective-permute-start(bf16[4,3,4,8,128]{4,3,2,1,0:T(8,128)(2,1)S(1)} %collective-permute-done.refs_1_), channel_id=1, source_target_pairs={{0,8},{8,0},{16,24},{24,16},{1,9},{9,1},{17,25},{25,17},{2,10},{10... | collective-permute-start | bytes 294920 | tf_op jit(solution)/shard_map/ppermute | solution.py:481
  16.8 1.3 %collective-permute-start.3 = (bf16[4,3,4,8,128]{4,3,2,1,0:T(8,128)(2,1)S(1)}, bf16[4,3,4,8,128]{4,3,2,1,0:T(8,128)(2,1)S(1)}, u32[]{:S(2)}, u32[]{:S(2)}) collective-permute-start(bf16[4,3,4,8,128]{4,3,2,1,0:T(8,128)(2,1)S(1)} %collective-permute-done.1.refs_2_), channel_id=1, source_target_pairs={{0,8},{8,0},{16,24},{24,16},{1,9},{9,1},{17,25},{25,17},{2,10},{10... | collective-permute-start | bytes 294920 | tf_op jit(solution)/shard_map/ppermute | solution.py:481
  17.7 0.6 %copy-start.3 = (bf16[4,3,4,8,128]{4,3,2,1,0:T(8,128)(2,1)}, bf16[4,3,4,8,128]{4,3,2,1,0:T(8,128)(2,1)S(1)}, u32[]{:S(2)}) copy-start(bf16[4,3,4,8,128]{4,3,2,1,0:T(8,128)(2,1)S(1)} %collective-permute-done.2.refs_3_) | copy-start | bytes 294916
  18.1 0.6 %copy-start.4 = (bf16[4,3,4,8,128]{4,3,2,1,0:T(8,128)(2,1)}, bf16[4,3,4,8,128]{4,3,2,1,0:T(8,128)(2,1)S(1)}, u32[]{:S(2)}) copy-start(bf16[4,3,4,8,128]{4,3,2,1,0:T(8,128)(2,1)S(1)} %collective-permute-done.3.refs_4_) | copy-start | bytes 294916

commit v3 on v2

--- a/solution.py
+++ b/solution.py
@@ -38,8 +38,15 @@
     return ((i & 1) << 7) | ((i >> 7) << 6) | ((i & 127) >> 1)
 
 
-def middle_order(i):
-    return (((i >> 6) & 1) << 8) | ((i & 1) << 7) | ((i >> 7) << 5) | ((i & 63) >> 1)
+def split_middle():
+    r, c = iotas(384, 512)
+    return chosen((((r & 1) << 8) | (((r >> 7) + 3 * ((r >> 6) & 1)) << 5) | ((r & 63) >> 1)) == c)
+
+
+def join_middle():
+    r, c = iotas(512, 640)
+    source = ((2 * ((r >> 5) & 3) + (r >> 8)) << 6) | ((r & 31) << 1) | ((r >> 7) & 1)
+    return chosen(source == ((((c >> 7) + 3 * ((c >> 6) & 1)) << 6) | (c & 63)))
 
 
 def coarse_tap(dz, dx):
@@ -52,10 +59,10 @@
     return chosen(col == ((r // 9 * 3 + c) * 3 + r % 3) * 16 + r // 3 % 3)
 
 
-def prep_kernel(lift, *refs):
+def prep_kernel(lift, head, *refs):
     sources, refs = refs[:5], refs[5:]
-    results, refs = refs[:13], refs[13:]
-    (t_o, wf_o, wf9_o, wd1_o, wm_o, wm9_o, wd2_o, wmf_o, sf_o, sft_o, sm_o, smt_o, st_o), refs = refs[:13], refs[13:]
+    results, refs = refs[:15], refs[15:]
+    (t_o, wf_o, wf9_o, wd1_o, wm_o, wm9_o, wd2_o, wmf_o, wmf9_o, sf_o, sft_o, sm_o, smt_o, st_o, head_o), refs = refs[:15], refs[15:]
     (fine, red1, mid, red2, mfine), sems, out_sems = refs[:5], refs[5], refs[6]
     copies = [pltpu.make_async_copy(src, dst, sems.at[i]) for i, (src, dst) in enumerate(zip(sources, refs))]
     for copy in copies:
@@ -63,9 +70,9 @@
     r, c = iotas(256, 256)
     sf_o[...] = chosen(fine_order(r) == c)
     sft_o[...] = chosen(r == fine_order(c))
-    r, c = iotas(512, 512)
-    sm_o[...] = chosen(middle_order(r) == c)
-    smt_o[...] = chosen(r == middle_order(c))
+    head_o[...] = jnp.concatenate([head[...].astype(F32), jnp.zeros((13, 32), F32)], axis=0).astype(BF)
+    sm_o[...] = split_middle()
+    smt_o[...] = join_middle()
     for t in range(9):
         st_o[:, 128 * t : 128 * t + 128] = coarse_tap(t // 3, t % 3)
     base = sum(
@@ -78,6 +85,7 @@
     for copy in copies:
         copy.wait()
     wf9_o[...] = jnp.zeros_like(wf9_o)
+    wmf9_o[...] = jnp.zeros_like(wmf9_o)
     for dz in range(3):
         for dy in range(3):
             for dx in range(3):
@@ -85,9 +93,14 @@
                 if k < 8:
                     wf_o[32 * dz : 32 * dz + 32, 32 * k : 32 * k + 32] = fine[9 * dy + 3 * dz + dx]
                 else:
+                    for zo in range(6):
+                        wf9_o[32 * zo : 32 * zo + 32, 32 * (dz + zo) : 32 * (dz + zo) + 32] = fine[9 * dy + 3 * dz + dx]
+                if k < 8:
+                    wmf_o[32 * dz : 32 * dz + 32, 64 * k : 64 * k + 64] = mfine[9 * dy + 3 * dz + dx]
+                else:
                     for zo in range(2):
-                        wf9_o[32 * zo : 32 * zo + 32, 32 * (dz + zo) : 32 * (dz + zo) + 32] = fine[9 * dy + 3 * dz + dx]
-                wmf_o[32 * dz : 32 * dz + 32, 64 * k : 64 * k + 64] = mfine[9 * dy + 3 * dz + dx]
+                        at = 64 * (dz + zo)
+                        wmf9_o[32 * zo : 32 * zo + 32, at : at + 64] = mfine[9 * dy + 3 * dz + dx]
                 j = 3 * dz + dx
                 if j < 8:
                     wm_o[64 * dy : 64 * dy + 64, 64 * j : 64 * j + 64] = mid[9 * dy + 3 * dz + dx]
@@ -95,7 +108,7 @@
                     wm9_o[:, 64 * dy : 64 * dy + 64] = mid[9 * dy + 3 * dz + dx]
     wd1_o[...] = red1[...].astype(F32).T.astype(BF)
     wd2_o[...] = red2[...].astype(F32).T.astype(BF)
-    made = (t_o, wf_o, wf9_o, wd1_o, wm_o, wm9_o, wd2_o, wmf_o, sf_o, sft_o, sm_o, smt_o, st_o)
+    made = (t_o, wf_o, wf9_o, wd1_o, wm_o, wm9_o, wd2_o, wmf_o, wmf9_o, sf_o, sft_o, sm_o, smt_o, st_o, head_o)
     copies = [pltpu.make_async_copy(src, dst, out_sems.at[i]) for i, (src, dst) in enumerate(zip(made, results))]
     for copy in copies:
         copy.start()
@@ -128,33 +141,24 @@
     )
 
 
-def shifted_rows(direct):
-    lane = lax.broadcasted_iota(jnp.int32, direct[0].shape, 1)
-    first = lane < 64
-    edges = (lane & 63) == 0, (lane & 63) == 63
-    kept, swapped = [], []
-    for v in direct:
-        t = pltpu.roll(v, 64, 1)
-        pairs = [(pltpu.roll(v, n, 1), pltpu.roll(t, n, 1)) for n in (1, 127)]
-        low, high = (jnp.where(edge, rt, rv) for edge, (rv, rt) in zip(edges, pairs))
-        low_t, high_t = (jnp.where(edge, rv, rt) for edge, (rv, rt) in zip(edges, pairs))
-        kept.append((low, v, high))
-        swapped.append((low_t, t, high_t))
-    result = []
-    for p in range(len(direct)):
-        result.append(kept[p])
-        if p + 1 < len(direct):
-            result.append(tuple(jnp.where(first, u, w) for u, w in zip(swapped[p], swapped[p + 1])))
-    return result
-
-
-def net_kernel(periodic, me, *refs):
+def half_shifts(v):
+    lane = lax.broadcasted_iota(jnp.int32, v.shape, 1) & 63
+    t = pltpu.roll(v, 64, 1)
+    low_v, low_t, high_v, high_t = (pltpu.roll(u, n, 1) for n in (1, 127) for u in (v, t))
+    low, high = lane == 0, lane == 63
+    return (
+        (jnp.where(low, low_t, low_v), v, jnp.where(high, high_t, high_v)),
+        (jnp.where(low, low_v, low_t), t, jnp.where(high, high_v, high_t)),
+    )
+
+
+def net_kernel(periodic, *refs):
     count = 5 if periodic else 1
     fields, refs = refs[:count], refs[count:]
-    head, weights, out, refs = refs[0], refs[1:18], refs[18], refs[19:]
-    pat, lifted, fine, halves, mskip, quarters, ctaps, ups, mout, joined = refs[:10]
-    held, sems = refs[10:27], refs[27]
-    near_by, field_sems = refs[28 : 28 + count], refs[28 + count]
+    weights, out, refs = refs[:19], refs[19], refs[20:]
+    pat, lifted, fine, halves, mskip, quarters, ctaps, ups, mout, joined, jfine = refs[:11]
+    held, sems = refs[11:30], refs[30]
+    near_by, field_sems = refs[31 : 31 + count], refs[31 + count]
     field_copies = [
         pltpu.make_async_copy(src, dst, field_sems.at[i]) for i, (src, dst) in enumerate(zip(fields, near_by))
     ]
@@ -166,14 +170,15 @@
         own, near, far, other_near, other_far = near_by
     else:
         wide = near_by[0]
-    (t_w, wf, wf9, s_fine, wd1, wm, wm9, s_mid, wd2, s_taps, ck, we2, s_mid_t, mmk, we1, s_fine_t, wmf) = held
+    (t_w, wf, wf9, s_fine, wd1, wm, wm9, s_mid, wd2, s_taps, ck, we2, s_mid_t, mmk, we1, s_fine_t, wmf, wmf9, head) = held
 
     def need(*names):
         for name in names:
             copies[[h is name for h in held].index(True)].wait()
 
     r_lin, r_lift, r_fine, r_mid, r_skip, r_coarse = levels(periodic)
-    core = lax.rem(me[0], 2)
+    me = lax.axis_index("gy")
+    core = lax.rem(me, 2)
 
     for copy in field_copies:
         copy.wait()
@@ -181,7 +186,7 @@
     def patch(k, carry):
         row = lax.rem(k, 4)
         if periodic:
-            block = lax.rem(me[0] + k // 4 + 2, 4)
+            block = lax.rem(me + k // 4 + 2, 4)
         for c in range(3):
             if periodic:
                 mine = [ref[block, c, row].astype(F32) for ref in (near, far)]
@@ -237,19 +242,16 @@
             parts += [r[:, :128], r[:, 128:]]
         rows = []
         last = [lifted[ys[2], 96 * z + 64 : 96 * z + 96] for z in range(30)]
-        for quad in range(7):
-            cols = [jnp.concatenate(last[4 * quad + 2 * h : 4 * quad + 2 * h + 4], axis=0) for h in range(2)]
-            r = dot(wf9[...], jnp.concatenate(cols, axis=1))
-            for i in range(4):
-                z, zo, h = 4 * quad + i, i % 2, i // 2
+        for first, outs in ((0, 6), (12, 6), (24, 2)):
+            cols = [jnp.concatenate(last[first + outs * h : first + outs * h + outs + 2], axis=0) for h in range(2)]
+            r = dot(wf9[: 32 * outs, : 32 * outs + 64], jnp.concatenate(cols, axis=1))
+            for i in range(2 * outs):
+                z, zo, h = first + i, i % outs, i // outs
                 v = parts[z][0:32] + parts[z + 1][32:64] + parts[z + 2][64:96]
                 v = act(v + r[32 * zo : 32 * zo + 32, 128 * h : 128 * h + 128]).astype(BF)
                 fine[k, z] = v
                 rows.append(v)
-        left = []
-        for p in range(7):
-            for b in range(2):
-                left.append(jnp.concatenate([rows[4 * p + b], rows[4 * p + 2 + b]], axis=1))
+        left = [jnp.concatenate([rows[z], rows[z + 14]], axis=1) for z in range(14)]
         s = dot(jnp.concatenate(left, axis=0), s_fine[...]).astype(BF)
         for i in range(14):
             for c in range(2):
@@ -272,11 +274,15 @@
             r = act(dot(wd1[...], jnp.concatenate(cols, axis=1)))
             for h in range(2):
                 direct[h].append(r[:, 128 * h : 128 * h + 128])
+        first = lax.broadcasted_iota(jnp.int32, (64, 128), 1) < 64
         for h in range(2):
-            for pos, triple in enumerate(shifted_rows(direct[h])):
-                for dx, u in enumerate(triple):
-                    at = pos * 192 + dx * 64
-                    lifted[2 * k + h, at : at + 64] = u.astype(BF)
+            kept, turned = zip(*(half_shifts(v.astype(BF)) for v in direct[h]))
+            lows = [*kept, turned[0]]
+            highs = [turned[6], *kept]
+            for q in range(8):
+                for dx in range(3):
+                    at = q * 192 + dx * 64
+                    lifted[2 * k + h, at : at + 64] = jnp.where(first, lows[q][dx], highs[q][dx])
         return carry
 
     lax.fori_loop(0, r_mid.count // 2, middle_in, 0)
@@ -285,7 +291,7 @@
 
     def middle_conv(k, carry):
         parts = []
-        start = pl.multiple_of(k * 384, 384)
+        start = pl.multiple_of(k * 192, 192)
         for pair in range(r_mid.count // 2):
             cols = [lifted[2 * pair + h, pl.ds(start, 512)] for h in range(2)]
             r = dot(wm[...], jnp.concatenate(cols, axis=1))
@@ -302,19 +308,34 @@
 
     lax.fori_loop(0, 6, middle_conv, 0, unroll=True)
 
-    need(s_mid, wd2, s_taps)
-
-    for chunk in range(2):
-        width = 4 if chunk == 0 else 2
-        left = [
-            jnp.concatenate([mskip[y, 4 * chunk + q] for q in range(width)], axis=1) for y in range(r_skip.count)
-        ]
-        s = dot(jnp.concatenate(left, axis=0), s_mid[: 128 * width]).astype(BF)
-        for y in range(r_skip.count):
-            for t in range(4):
-                quarters[y, t * 64 : t * 64 + 64, 128 * chunk : 128 * chunk + 128] = s[
-                    64 * y : 64 * y + 64, 128 * t : 128 * t + 128
-                ]
+    need(s_mid, wd2, s_taps, ck, we2, s_mid_t, mmk, we1, s_fine_t, wmf, wmf9, head)
+
+    first = lax.broadcasted_iota(jnp.int32, (64, 128), 1) < 64
+    for y in range(6):
+        skip = [mskip[r_skip.at(y - 2), q].astype(F32) for q in range(6)]
+        turned = {q: pltpu.roll(skip[q], 64, 1) for q in (0, 5)}
+        lows = [skip[2], skip[3], skip[4], skip[5], turned[0]]
+        highs = [turned[5], skip[0], skip[1], skip[2], skip[3]]
+        for q in range(5):
+            for dx, u in enumerate(half_shifts(jnp.where(first, lows[q], highs[q]))[0]):
+                at = q * 384 + dx * 128 + 64
+                joined[y, at : at + 64] = u.astype(BF)
+    for y in range(6):
+        for z in range(10):
+            v = fine[r_fine.at(y - 1), z + 9].astype(F32)
+            for dx, u in enumerate((pltpu.roll(v, 1, 1), v, pltpu.roll(v, 127, 1))):
+                at = 192 * z + 64 * dx + 32
+                jfine[y, at : at + 32] = u.astype(BF)
+
+    left = [
+        jnp.concatenate([mskip[y, 2 * j + b] for j in range(3)], axis=1) for y in range(r_skip.count) for b in range(2)
+    ]
+    s = dot(jnp.concatenate(left, axis=0), s_mid[...]).astype(BF)
+    for y in range(r_skip.count):
+        for b in range(2):
+            for c in range(2):
+                at = (2 * b + c) * 64
+                quarters[y, at : at + 64] = s[64 * (2 * y + b) : 64 * (2 * y + b) + 64, 256 * c : 256 * c + 256]
     cin = []
     for y in range(r_coarse.count):
         rel = 2 * (y + r_coarse.low)
@@ -324,8 +345,6 @@
     for y in range(r_coarse.count):
         for t in range(9):
             ctaps[y, 128 * t : 128 * t + 128] = taps[128 * y : 128 * y + 128, 128 * t : 128 * t + 128]
-
-    need(ck, we2, s_mid_t)
 
     wc = jnp.concatenate([ck[t] for t in range(27)], axis=1)
     for first in (-1, 1):
@@ -340,19 +359,14 @@
                 rows.append(jnp.concatenate(blocks, axis=1))
         s = dot(jnp.concatenate(rows, axis=0), s_mid_t[...]).astype(BF)
         for i in range(len(rows)):
-            for q in range(4):
+            for q in range(5):
                 ups[2 * (first + 1) + i, q] = s[64 * i : 64 * i + 64, 128 * q : 128 * q + 128]
 
-    need(mmk)
-
     for y in range(6):
-        direct = [
-            jnp.concatenate([ups[y, q], mskip[r_skip.at(y - 2), q + 1]], axis=0).astype(F32) for q in range(4)
-        ]
-        for pos, triple in enumerate(shifted_rows(direct)):
-            for dx, u in enumerate(triple):
-                at = pos * 384 + dx * 128
-                joined[y, at : at + 128] = u.astype(BF)
+        for q in range(5):
+            for dx, u in enumerate(half_shifts(ups[y, q].astype(F32))[0]):
+                at = q * 384 + dx * 128
+                joined[y, at : at + 64] = u.astype(BF)
     wmm = jnp.concatenate(
         [
             jnp.concatenate([mmk[9 * dy + 3 * dz + dx] for dz in range(3) for dx in range(3)], axis=1)
@@ -363,14 +377,12 @@
     for k in range(3):
         parts = []
         for pair in range(3):
-            cols = [joined[2 * pair + h, 768 * k : 768 * k + 1152] for h in range(2)]
+            cols = [joined[2 * pair + h, 384 * k : 384 * k + 1152] for h in range(2)]
             r = dot(wmm, jnp.concatenate(cols, axis=1))
             parts += [r[:, :128], r[:, 128:]]
         for y in range(4):
             v = parts[y][0:64] + parts[y + 1][64:128] + parts[y + 2][128:192]
             mout[y, k] = act(v).astype(BF)
-
-    need(we1, s_fine_t)
 
     for y in range(4):
         for k in range(3):
@@ -385,28 +397,33 @@
                     continue
                 for b in range(2):
                     for h in range(2):
-                        zf = -2 + 4 * k + 2 * h + b
+                        zf = -2 + 2 * k + b + 6 * h
                         if not -1 <= zf <= 8:
                             continue
                         up = s[(2 * a + b) * 32 : (2 * a + b) * 32 + 32, 128 * h : 128 * h + 128]
-                        skip = fine[r_fine.at(yf), zf + 10].astype(F32)
-                        v = jnp.concatenate([up, skip], axis=0)
-                        lifted[yf + 1, 192 * (zf + 1) + 0 : 192 * (zf + 1) + 64] = pltpu.roll(v, 1, 1).astype(BF)
-                        lifted[yf + 1, 192 * (zf + 1) + 64 : 192 * (zf + 1) + 128] = v.astype(BF)
-                        lifted[yf + 1, 192 * (zf + 1) + 128 : 192 * (zf + 1) + 192] = pltpu.roll(v, 127, 1).astype(BF)
-
-    need(wmf)
+                        for dx, u in enumerate((pltpu.roll(up, 1, 1), up, pltpu.roll(up, 127, 1))):
+                            at = 192 * (zf + 1) + 64 * dx
+                            jfine[yf + 1, at : at + 32] = u.astype(BF)
 
     for y in range(4):
         parts = []
         for pair in range(5):
-            cols = [jnp.concatenate([lifted[y + dy, 192 * (2 * pair + h) : 192 * (2 * pair + h) + 192] for dy in range(3)], axis=0) for h in range(2)]
+            cols = []
+            for h in range(2):
+                at = 192 * (2 * pair + h)
+                rows = [jfine[y, at : at + 192], jfine[y + 1, at : at + 192], jfine[y + 2, at : at + 128]]
+                cols.append(jnp.concatenate(rows, axis=0))
             r = dot(wmf[...], jnp.concatenate(cols, axis=1))
             parts += [r[:, :128], r[:, 128:]]
+        last = [jfine[y + 2, 192 * z + 128 : 192 * z + 192] for z in range(10)]
         rows = []
-        for z in range(8):
-            v = parts[z][0:32] + parts[z + 1][32:64] + parts[z + 2][64:96]
-            rows.append(act(v).astype(BF))
+        for quad in range(2):
+            cols = [jnp.concatenate(last[4 * quad + 2 * h : 4 * quad + 2 * h + 4], axis=0) for h in range(2)]
+            r = dot(wmf9[...], jnp.concatenate(cols, axis=1))
+            for i in range(4):
+                z, zo, h = 4 * quad + i, i % 2, i // 2
+                v = parts[z][0:32] + parts[z + 1][32:64] + parts[z + 2][64:96]
+                rows.append(act(v + r[32 * zo : 32 * zo + 32, 128 * h : 128 * h + 128]).astype(BF))
         d = dot(head[...], jnp.concatenate(rows, axis=1))
         for z in range(8):
             for o in range(3):
@@ -442,29 +459,31 @@
     forms = [
         (256, 432),
         (96, 256),
-        (64, 128),
+        (192, 256),
         (64, 256),
         (192, 512),
         (64, 192),
         (128, 512),
-        (96, 576),
+        (96, 512),
+        (64, 256),
         (256, 256),
         (256, 256),
-        (512, 512),
-        (512, 512),
+        (384, 512),
+        (512, 640),
         (256, 1152),
+        (16, 32),
     ]
     prepared = pl.pallas_call(
         prep_kernel,
         out_shape=[jax.ShapeDtypeStruct(s, BF) for s in forms],
-        in_specs=[VMEM] + [HBM] * len(raw),
+        in_specs=[VMEM, VMEM] + [HBM] * len(raw),
         out_specs=[HBM] * len(forms),
         scratch_shapes=[pltpu.VMEM(s, BF) for s in forms]
         + [pltpu.VMEM(w.shape, BF) for w in raw]
         + [pltpu.SemaphoreType.DMA((len(raw),)), pltpu.SemaphoreType.DMA((len(forms),))],
         cost_estimate=pl.CostEstimate(flops=4_000_000_000, bytes_accessed=10_000_000, transcendentals=0),
         compiler_params=pltpu.CompilerParams(vmem_limit_bytes=60 << 20),
-    )(lift_kernel.transpose(2, 0, 1), *raw)
+    )(lift_kernel.transpose(2, 0, 1), output_head, *raw)
     count_y, count_z = lax.axis_size("gy"), lax.axis_size("gz")
     periodic = count_y == 4
     if periodic:
@@ -489,9 +508,8 @@
         fields = [
             jnp.stack([wide if h == 0 else lax.ppermute(wide, "gy", ring("gy", -h)) for h in range(-3, 4)])
         ]
-    me = lax.axis_index("gy").astype(jnp.int32).reshape(1)
-
-    t_w, wf, wf9, wd1, wm, wm9, wd2, wmf, split_f, split_ft, split_m, split_mt, taps = prepared
+
+    t_w, wf, wf9, wd1, wm, wm9, wd2, wmf, wmf9, split_f, split_ft, split_m, split_mt, taps, head = prepared
 
     r_lin, r_lift, r_fine, r_mid, r_skip, r_coarse = levels(periodic)
     scratch = [
@@ -502,9 +520,10 @@
         pltpu.VMEM((r_skip.count, 6, 64, 128), BF),
         pltpu.VMEM((r_skip.count, 256, 256), BF),
         pltpu.VMEM((r_coarse.count, 1152, 128), BF),
-        pltpu.VMEM((6, 4, 64, 128), BF),
+        pltpu.VMEM((6, 5, 64, 128), BF),
         pltpu.VMEM((4, 3, 64, 128), BF),
-        pltpu.VMEM((6, 7 * 384, 128), BF),
+        pltpu.VMEM((6, 5 * 384, 128), BF),
+        pltpu.VMEM((6, 10 * 192, 128), BF),
     ]
     weights = [
         t_w,
@@ -524,6 +543,8 @@
         expand_first.reshape(256, 64),
         split_ft,
         wmf,
+        wmf9,
+        head,
     ]
     scratch += [pltpu.VMEM(w.shape, BF) for w in weights]
     scratch.append(pltpu.SemaphoreType.DMA((len(weights),)))
@@ -531,11 +552,11 @@
     return pl.pallas_call(
         functools.partial(net_kernel, periodic),
         out_shape=jax.ShapeDtypeStruct(linear_field.shape, F32),
-        in_specs=[SMEM] + [ANY] * len(fields) + [VMEM] + [HBM] * len(weights),
+        in_specs=[ANY] * len(fields) + [HBM] * len(weights),
         out_specs=VMEM,
         scratch_shapes=scratch,
         compiler_params=pltpu.CompilerParams(vmem_limit_bytes=60 << 20),
-    )(me, *fields, output_head, *weights)
+    )(*fields, *weights)
 
 
 def solution(mesh):

time: 45.2 us -> 43.3 us (0.958)
  Pallas kernels: 31 us -> 29.1 us
    pallas_call x1, Pallas kernels: 26.1 us -> 24.1 us  [body(): pl.pallas_call(functools.partial(net_kernel, periodic), out_shape=jax.Sha...]
  transfers between devices with their start and end apart: 4 -> 4, of which waited for: 3 -> 3; matrix products, arithmetic and copies ran while one was open for 0% -> 0% of each run, Pallas kernels for 11% -> 12%
where the time goes in v3:
time: 43.3 us; the launch traced here: 43.1 us
  Pallas kernels  29.1 us (67%)
  blocking collectives  6.53 us (15%)
  starting transfers between devices  4.52 us (10%)
  waiting for transfers between devices  2.08 us (5%)
  local copies, waits for them, and re-layouts  0.64 us (1%)
    pallas_call x1, Pallas kernels, body(): pl.pallas_call(functools.partial(net_kernel, periodic), out_shape=jax.Sha...  24.1 us
    all_gather x1, blocking collectives, body(): own = lax.all_gather(linear_field, 'gy')  6.53 us
    pallas_call x1, Pallas kernels, body(): pl.pallas_call(prep_kernel, out_shape=[jax.ShapeDtypeStruct(s, BF) for s...  5.09 us
    ppermute x2, starting transfers between devices, body(): sides.append(lax.ppermute(own, ('gy', 'gz'), pairs))  3.51 us
    ppermute x2, waiting for transfers between devices, body(): fields = [own, *sides, *(lax.ppermute(side, 'gy', swap) for side in sides)]  1.22 us
    ppermute x2, starting transfers between devices, body(): fields = [own, *sides, *(lax.ppermute(side, 'gy', swap) for side in sides)]  1 us
  transfers between devices with their start and end apart: 4, of which 3 were waited for; matrix products, arithmetic and copies ran while one was open for 0% of the time, Pallas kernels for 12%

profile of v3, /device:TPU:0, one launch (start us, length us, event | category | flops | bytes accessed | tf_op | source)
XLA Modules:
  0.0 43.1 jit_solution(12361558967625195728)
XLA Ops:
  0.0 6.5 %all-gather = bf16[12,4,8,128]{3,2,1,0:T(8,128)(2,1)S(1)} all-gather(bf16[3,4,8,128]{3,2,1,0:T(8,128)(2,1)} %param.12), channel_id=2, replica_groups=mesh['gy'=4,'gz'=8] {'gy'}, dimensions={0}, use_global_device_ids=true | all-gather | bytes 122880 | tf_op jit(solution)/shard_map/all_gather | solution.py:490
  6.5 0.0 copy-start
  6.5 2.0 %collective-permute-start.1 = (bf16[4,3,4,8,128]{4,3,2,1,0:T(8,128)(2,1)S(1)}, bf16[4,3,4,8,128]{4,3,2,1,0:T(8,128)(2,1)S(1)}, u32[]{:S(2)}, u32[]{:S(2)}) collective-permute-start(bf16[4,3,4,8,128]{4,3,2,1,0:T(8,128)(2,1)S(1)} %bitcast.10), channel_id=1, source_target_pairs={{6,0},{7,1},{0,2},{1,3},{2,4},{3,5},{4,6},{5,7},{10,8},{11,9},{12,... | collective-permute-start | bytes 294920 | tf_op jit(solution)/shard_map/ppermute | solution.py:497
  8.6 1.5 %collective-permute-start = (bf16[4,3,4,8,128]{4,3,2,1,0:T(8,128)(2,1)S(1)}, bf16[4,3,4,8,128]{4,3,2,1,0:T(8,128)(2,1)S(1)}, u32[]{:S(2)}, u32[]{:S(2)}) collective-permute-start(bf16[4,3,4,8,128]{4,3,2,1,0:T(8,128)(2,1)S(1)} %bitcast.11), channel_id=1, source_target_pairs={{7,0},{0,1},{1,2},{2,3},{3,4},{4,5},{5,6},{6,7},{9,8},{10,9},{11,1... | collective-permute-start | bytes 294920 | tf_op jit(solution)/shard_map/ppermute | solution.py:497
  10.1 5.1 %shard_map.118 = (bf16[256,432]{1,0:T(8,128)(2,1)}, bf16[96,256]{1,0:T(8,128)(2,1)}, bf16[192,256]{1,0:T(8,128)(2,1)}, bf16[64,256]{1,0:T(8,128)(2,1)}, bf16[192...) custom-call(bf16[3,27,32]{2,1,0:T(8,128)(2,1)} %bitcast.17, ...), custom_call_target="tpu_custom_call" | custom-call | flops 4000000000 | bytes 10000000 | tf_op jit(solution)/shard_map/pallas_call | solution.py:476
  15.1 0.0 copy-done
  15.2 0.0 collective-permute-done.1.refs_2_
  15.2 0.0 copy-start.1
  15.2 0.9 %collective-permute-done.refs_1_ = bf16[4,3,4,8,128]{4,3,2,1,0:T(8,128)(2,1)S(1)} collective-permute-done((bf16[4,3,4,8,128]{4,3,2,1,0:T(8,128)(2,1)S(1)}, bf16[4,3,4,8,128]{4,3,2,1,0:T(8,128)(2,1)S(1)}, u32[]{:S(2)}, u32[]{:S(2)}) %collective-permute-start) | collective-permute-done | bytes 98336 | tf_op jit(solution)/shard_map/ppermute | solution.py:497
  16.0 0.0 copy-start.2
  16.0 0.9 %collective-permute-start.2 = (bf16[4,3,4,8,128]{4,3,2,1,0:T(8,128)(2,1)S(1)}, bf16[4,3,4,8,128]{4,3,2,1,0:T(8,128)(2,1)S(1)}, u32[]{:S(2)}, u32[]{:S(2)}) collective-permute-start(bf16[4,3,4,8,128]{4,3,2,1,0:T(8,128)(2,1)S(1)} %collective-permute-done.refs_1_), channel_id=1, source_target_pairs={{0,8},{8,0},{16,24},{24,16},{1,9},{9,1},{17,25},{25,17},{2,10},{10... | collective-permute-start | bytes 294920 | tf_op jit(solution)/shard_map/ppermute | solution.py:500
  17.0 0.1 collective-permute-start.3
  17.0 0.9 %collective-permute-done.2.refs_3_ = bf16[4,3,4,8,128]{4,3,2,1,0:T(8,128)(2,1)S(1)} collective-permute-done((bf16[4,3,4,8,128]{4,3,2,1,0:T(8,128)(2,1)S(1)}, bf16[4,3,4,8,128]{4,3,2,1,0:T(8,128)(2,1)S(1)}, u32[]{:S(2)}, u32[]{:S(2)}) %collective-permute-start.2) | collective-permute-done | bytes 98336 | tf_op jit(solution)/shard_map/ppermute | solution.py:500
  17.9 0.0 copy-start.3
  17.9 0.4 collective-permute-done.3.refs_4_
  18.3 0.0 copy-start.4
  18.3 0.0 copy-done.1
  18.3 0.0 copy-done.2
  18.3 0.3 copy-done.3
  18.5 0.4 copy-done.4
  18.9 24.1 %shard_map.119 = f32[3,4,8,128]{3,2,1,0:T(8,128)} custom-call(bf16[4,3,4,8,128]{4,3,2,1,0:T(8,128)(2,1)} %bitcast.12, bf16[4,3,4,8,128]{4,3,2,1,0:T(8,128)(2,1)} %copy-done.2, bf16[4,3,4,8,128]{4,3,2,1,0:T(8,128)(2,1)} %copy-done.1, bf16[4,3,4,8,128]{4,3,2,1,0:T(8,128)(2,1)} %copy-done.3, bf16[4,3,4,8,128]{4,3,2,1,0:T(8,128)(2,1)} %copy-done.4, ...), custom_call_target="tpu_custom_call" | custom-call | tf_op jit(solution)/shard_map/pallas_call | solution.py:552
Async XLA Ops:
  6.5 8.6 %copy-start = (bf16[12,4,8,128]{3,2,1,0:T(8,128)(2,1)}, bf16[12,4,8,128]{3,2,1,0:T(8,128)(2,1)S(1)}, u32[]{:S(2)}) copy-start(bf16[12,4,8,128]{3,2,1,0:T(8,128)(2,1)S(1)} %all-gather) | copy-start | bytes 294916
  6.5 8.6 %collective-permute-start.1 = (bf16[4,3,4,8,128]{4,3,2,1,0:T(8,128)(2,1)S(1)}, bf16[4,3,4,8,128]{4,3,2,1,0:T(8,128)(2,1)S(1)}, u32[]{:S(2)}, u32[]{:S(2)}) collective-permute-start(bf16[4,3,4,8,128]{4,3,2,1,0:T(8,128)(2,1)S(1)} %bitcast.10), channel_id=1, source_target_pairs={{6,0},{7,1},{0,2},{1,3},{2,4},{3,5},{4,6},{5,7},{10,8},{11,9},{12,... | collective-permute-start | bytes 294920 | tf_op jit(solution)/shard_map/ppermute | solution.py:497
  8.6 7.5 %collective-permute-start = (bf16[4,3,4,8,128]{4,3,2,1,0:T(8,128)(2,1)S(1)}, bf16[4,3,4,8,128]{4,3,2,1,0:T(8,128)(2,1)S(1)}, u32[]{:S(2)}, u32[]{:S(2)}) collective-permute-start(bf16[4,3,4,8,128]{4,3,2,1,0:T(8,128)(2,1)S(1)} %bitcast.11), channel_id=1, source_target_pairs={{7,0},{0,1},{1,2},{2,3},{3,4},{4,5},{5,6},{6,7},{9,8},{10,9},{11,1... | collective-permute-start | bytes 294920 | tf_op jit(solution)/shard_map/ppermute | solution.py:497
  15.2 3.1 %copy-start.1 = (bf16[4,3,4,8,128]{4,3,2,1,0:T(8,128)(2,1)}, bf16[4,3,4,8,128]{4,3,2,1,0:T(8,128)(2,1)S(1)}, u32[]{:S(2)}) copy-start(bf16[4,3,4,8,128]{4,3,2,1,0:T(8,128)(2,1)S(1)} %collective-permute-done.1.refs_2_) | copy-start | bytes 294916
  16.0 2.2 %copy-start.2 = (bf16[4,3,4,8,128]{4,3,2,1,0:T(8,128)(2,1)}, bf16[4,3,4,8,128]{4,3,2,1,0:T(8,128)(2,1)S(1)}, u32[]{:S(2)}) copy-start(bf16[4,3,4,8,128]{4,3,2,1,0:T(8,128)(2,1)S(1)} %collective-permute-done.refs_1_) | copy-start | bytes 294916
  16.0 1.9 %collective-permute-start.2 = (bf16[4,3,4,8,128]{4,3,2,1,0:T(8,128)(2,1)S(1)}, bf16[4,3,4,8,128]{4,3,2,1,0:T(8,128)(2,1)S(1)}, u32[]{:S(2)}, u32[]{:S(2)}) collective-permute-start(bf16[4,3,4,8,128]{4,3,2,1,0:T(8,128)(2,1)S(1)} %collective-permute-done.refs_1_), channel_id=1, source_target_pairs={{0,8},{8,0},{16,24},{24,16},{1,9},{9,1},{17,25},{25,17},{2,10},{10... | collective-permute-start | bytes 294920 | tf_op jit(solution)/shard_map/ppermute | solution.py:500
  17.0 1.3 %collective-permute-start.3 = (bf16[4,3,4,8,128]{4,3,2,1,0:T(8,128)(2,1)S(1)}, bf16[4,3,4,8,128]{4,3,2,1,0:T(8,128)(2,1)S(1)}, u32[]{:S(2)}, u32[]{:S(2)}) collective-permute-start(bf16[4,3,4,8,128]{4,3,2,1,0:T(8,128)(2,1)S(1)} %collective-permute-done.1.refs_2_), channel_id=1, source_target_pairs={{0,8},{8,0},{16,24},{24,16},{1,9},{9,1},{17,25},{25,17},{2,10},{10... | collective-permute-start | bytes 294920 | tf_op jit(solution)/shard_map/ppermute | solution.py:500
  17.9 0.6 %copy-start.3 = (bf16[4,3,4,8,128]{4,3,2,1,0:T(8,128)(2,1)}, bf16[4,3,4,8,128]{4,3,2,1,0:T(8,128)(2,1)S(1)}, u32[]{:S(2)}) copy-start(bf16[4,3,4,8,128]{4,3,2,1,0:T(8,128)(2,1)S(1)} %collective-permute-done.2.refs_3_) | copy-start | bytes 294916
  18.3 0.6 %copy-start.4 = (bf16[4,3,4,8,128]{4,3,2,1,0:T(8,128)(2,1)}, bf16[4,3,4,8,128]{4,3,2,1,0:T(8,128)(2,1)S(1)}, u32[]{:S(2)}) copy-start(bf16[4,3,4,8,128]{4,3,2,1,0:T(8,128)(2,1)S(1)} %collective-permute-done.3.refs_4_) | copy-start | bytes 294916

commit v4 on v3

--- a/solution.py
+++ b/solution.py
@@ -156,9 +156,9 @@
     count = 5 if periodic else 1
     fields, refs = refs[:count], refs[count:]
     weights, out, refs = refs[:19], refs[19], refs[20:]
-    pat, lifted, fine, halves, mskip, quarters, ctaps, ups, mout, joined, jfine = refs[:11]
-    held, sems = refs[11:30], refs[30]
-    near_by, field_sems = refs[31 : 31 + count], refs[31 + count]
+    pat, lifted, fine, halves, mskip, quarters, ctaps, ups, mout, joined, jfine, mids = refs[:12]
+    held, sems = refs[12:31], refs[31]
+    near_by, field_sems = refs[32 : 32 + count], refs[32 + count]
     field_copies = [
         pltpu.make_async_copy(src, dst, field_sems.at[i]) for i, (src, dst) in enumerate(zip(fields, near_by))
     ]
@@ -184,26 +184,28 @@
         copy.wait()
 
     def patch(k, carry):
-        row = lax.rem(k, 4)
-        if periodic:
-            block = lax.rem(me + k // 4 + 2, 4)
         for c in range(3):
             if periodic:
-                mine = [ref[block, c, row].astype(F32) for ref in (near, far)]
-                others = [ref[block, c, row].astype(F32) for ref in (other_near, other_far)]
-                below_1, below_2 = (jnp.where(core == 0, m, t) for m, t in zip(mine, others))
-                above_1, above_2 = (jnp.where(core == 0, t, m) for m, t in zip(mine, others))
-                parts = [below_2[4:], below_1, own[block, c, row].astype(F32), above_1, above_2[:4]]
-                mid_v = jnp.concatenate(parts, axis=0)
-            else:
-                mid_v = wide[k // 4, c, row].astype(F32)
-            for dx, v in enumerate((pltpu.roll(mid_v, 1, 1), mid_v, pltpu.roll(mid_v, 127, 1))):
-                v = jnp.concatenate([v, jnp.zeros((8, 128), F32)], axis=0)
-                for j in range(4):
-                    pat[k, j, (3 * c + dx) * 16 : (3 * c + dx) * 16 + 16] = v[8 * j : 8 * j + 16].astype(BF)
+                block = lax.rem(me + k + 2, 4)
+                mine, by, away, other_by, other_away = (
+                    ref[block, c].astype(F32) for ref in (own, near, far, other_near, other_far)
+                )
+                below = jnp.where(core == 0, by, other_by), jnp.where(core == 0, away, other_away)
+                above = jnp.where(core == 0, other_by, by), jnp.where(core == 0, other_away, away)
+            for row in range(4):
+                if periodic:
+                    at = slice(8 * row, 8 * row + 8)
+                    parts = [below[1][at][4:], below[0][at], mine[at], above[0][at], above[1][at][:4]]
+                    v = jnp.concatenate([*parts, jnp.zeros((8, 128), F32)], axis=0)
+                else:
+                    v = jnp.concatenate([wide[k, c, row].astype(F32), jnp.zeros((8, 128), F32)], axis=0)
+                for dx, u in enumerate((pltpu.roll(v, 1, 1), v, pltpu.roll(v, 127, 1))):
+                    for j in range(4):
+                        at_k = (3 * c + dx) * 16
+                        pat[4 * k + row, j, at_k : at_k + 16] = u[8 * j : 8 * j + 16].astype(BF)
         return carry
 
-    lax.fori_loop(0, r_lin.count, patch, 0, unroll=8)
+    lax.fori_loop(0, r_lin.count // 4, patch, 0, unroll=2 if periodic else 1)
     for copy in copies[1:]:
         copy.start()
 
@@ -227,7 +229,7 @@
 
     lax.fori_loop(0, r_lift.count, lift, 0, unroll=8)
 
-    need(wf, wf9, s_fine)
+    need(wf, wf9, s_fine, wd1)
 
     def fine_conv(k, carry):
         rel = k + r_fine.low
@@ -260,10 +262,6 @@
                 ]
         return carry
 
-    lax.fori_loop(0, r_fine.count, fine_conv, 0, unroll=8)
-
-    need(wd1)
-
     def middle_in(k, carry):
         direct = [[], []]
         for p in range(7):
@@ -282,10 +280,15 @@
             for q in range(8):
                 for dx in range(3):
                     at = q * 192 + dx * 64
-                    lifted[2 * k + h, at : at + 64] = jnp.where(first, lows[q][dx], highs[q][dx])
+                    mids[2 * k + h, at : at + 64] = jnp.where(first, lows[q][dx], highs[q][dx])
         return carry
 
-    lax.fori_loop(0, r_mid.count // 2, middle_in, 0)
+    def down(k, carry):
+        for j in range(4):
+            fine_conv(4 * k + j, carry)
+        return middle_in(k, carry)
+
+    lax.fori_loop(0, r_mid.count // 2, down, 0, unroll=4 if periodic else 1)
 
     need(wm, wm9)
 
@@ -293,10 +296,10 @@
         parts = []
         start = pl.multiple_of(k * 192, 192)
         for pair in range(r_mid.count // 2):
-            cols = [lifted[2 * pair + h, pl.ds(start, 512)] for h in range(2)]
+            cols = [mids[2 * pair + h, pl.ds(start, 512)] for h in range(2)]
             r = dot(wm[...], jnp.concatenate(cols, axis=1))
             parts += [r[:, :128], r[:, 128:]]
-        last = [lifted[y, pl.ds(start + 512, 64)] for y in range(r_mid.count)]
+        last = [mids[y, pl.ds(start + 512, 64)] for y in range(r_mid.count)]
         for pair in range(r_skip.count // 2):
             rels = [2 * pair + h + r_skip.low for h in range(2)]
             cols = [jnp.concatenate([last[r_mid.at(rel + dy)] for dy in (-1, 0, 1)], axis=0) for rel in rels]
@@ -487,7 +490,7 @@
     count_y, count_z = lax.axis_size("gy"), lax.axis_size("gz")
     periodic = count_y == 4
     if periodic:
-        own = lax.all_gather(linear_field, "gy")
+        own = lax.all_gather(linear_field.reshape(3, 32, 128), "gy")
         sides = []
         for hops in (1, 2):
             pairs = []
@@ -524,6 +527,7 @@
         pltpu.VMEM((4, 3, 64, 128), BF),
         pltpu.VMEM((6, 5 * 384, 128), BF),
         pltpu.VMEM((6, 10 * 192, 128), BF),
+        pltpu.VMEM((r_mid.count, 8 * 192, 128), BF),
     ]
     weights = [
         t_w,

time: 43.3 us -> 42.2 us (0.975)
  Pallas kernels: 29.1 us -> 27.9 us
    pallas_call x1, Pallas kernels: 24.1 us -> 22.9 us  [body(): pl.pallas_call(functools.partial(net_kernel, periodic), out_shape=jax.Sha...]
where the time goes in v4:
time: 42.2 us; the launch traced here: 41.9 us
  Pallas kernels  27.9 us (66%)
  blocking collectives  6.53 us (15%)
  starting transfers between devices  4.52 us (11%)
  waiting for transfers between devices  2.08 us (5%)
  local copies, waits for them, and re-layouts  0.64 us (2%)
    pallas_call x1, Pallas kernels, body(): pl.pallas_call(functools.partial(net_kernel, periodic), out_shape=jax.Sha...  22.9 us
    all_gather x1, blocking collectives, body(): own = lax.all_gather(linear_field.reshape(3, 32, 128), 'gy')  6.53 us
    pallas_call x1, Pallas kernels, body(): pl.pallas_call(prep_kernel, out_shape=[jax.ShapeDtypeStruct(s, BF) for s...  5.09 us
    ppermute x2, starting transfers between devices, body(): sides.append(lax.ppermute(own, ('gy', 'gz'), pairs))  3.51 us
    ppermute x2, waiting for transfers between devices, body(): fields = [own, *sides, *(lax.ppermute(side, 'gy', swap) for side in sides)]  1.22 us
    ppermute x2, starting transfers between devices, body(): fields = [own, *sides, *(lax.ppermute(side, 'gy', swap) for side in sides)]  1 us
    ppermute x2, waiting for transfers between devices, body(): sides.append(lax.ppermute(own, ('gy', 'gz'), pairs))  0.86 us
  transfers between devices with their start and end apart: 4, of which 3 were waited for; matrix products, arithmetic and copies ran while one was open for 0% of the time, Pallas kernels for 12%

profile of v4, /device:TPU:0, one launch (start us, length us, event | category | flops | bytes accessed | tf_op | source)
XLA Modules:
  0.0 41.9 jit_solution(173049227204326329)
XLA Ops:
  0.0 6.5 %all_gather.3.refs_0_ = bf16[4,3,32,128]{3,2,1,0:T(8,128)(2,1)S(1)} all-gather(bf16[1,3,32,128]{3,2,1,0:T(8,128)(2,1)} %bitcast.12), channel_id=1, replica_groups=mesh['gy'=4,'gz'=8] {'gy'}, dimensions={0}, use_global_device_ids=true | all-gather | bytes 122880 | tf_op jit(solution)/shard_map/all_gather | solution.py:493
  6.5 0.0 copy-start
  6.5 2.0 %collective-permute-start.1 = (bf16[4,3,32,128]{3,2,1,0:T(8,128)(2,1)S(1)}, bf16[4,3,32,128]{3,2,1,0:T(8,128)(2,1)S(1)}, u32[]{:S(2)}, u32[]{:S(2)}) collective-permute-start(bf16[4,3,32,128]{3,2,1,0:T(8,128)(2,1)S(1)} %all_gather.3.refs_0_), channel_id=1, source_target_pairs={{6,0},{7,1},{0,2},{1,3},{2,4},{3,5},{4,6},{5,7},{10,8},{11,9},{12,... | collective-permute-start | bytes 294920 | tf_op jit(solution)/shard_map/ppermute | solution.py:500
  8.6 1.5 %collective-permute-start = (bf16[4,3,32,128]{3,2,1,0:T(8,128)(2,1)S(1)}, bf16[4,3,32,128]{3,2,1,0:T(8,128)(2,1)S(1)}, u32[]{:S(2)}, u32[]{:S(2)}) collective-permute-start(bf16[4,3,32,128]{3,2,1,0:T(8,128)(2,1)S(1)} %all_gather.3.refs_0_), channel_id=1, source_target_pairs={{7,0},{0,1},{1,2},{2,3},{3,4},{4,5},{5,6},{6,7},{9,8},{10,9},{11,1... | collective-permute-start | bytes 294920 | tf_op jit(solution)/shard_map/ppermute | solution.py:500
  10.1 5.1 %shard_map.118 = (bf16[256,432]{1,0:T(8,128)(2,1)}, bf16[96,256]{1,0:T(8,128)(2,1)}, bf16[192,256]{1,0:T(8,128)(2,1)}, bf16[64,256]{1,0:T(8,128)(2,1)}, bf16[192...) custom-call(bf16[3,27,32]{2,1,0:T(8,128)(2,1)} %bitcast.15, ...), custom_call_target="tpu_custom_call" | custom-call | flops 4000000000 | bytes 10000000 | tf_op jit(solution)/shard_map/pallas_call | solution.py:479
  15.1 0.0 copy-done
  15.2 0.0 collective-permute-done.1.refs_2_
  15.2 0.0 copy-start.1
  15.2 0.9 %collective-permute-done.refs_1_ = bf16[4,3,32,128]{3,2,1,0:T(8,128)(2,1)S(1)} collective-permute-done((bf16[4,3,32,128]{3,2,1,0:T(8,128)(2,1)S(1)}, bf16[4,3,32,128]{3,2,1,0:T(8,128)(2,1)S(1)}, u32[]{:S(2)}, u32[]{:S(2)}) %collective-permute-start) | collective-permute-done | bytes 98336 | tf_op jit(solution)/shard_map/ppermute | solution.py:500
  16.0 0.0 copy-start.2
  16.0 0.9 %collective-permute-start.2 = (bf16[4,3,32,128]{3,2,1,0:T(8,128)(2,1)S(1)}, bf16[4,3,32,128]{3,2,1,0:T(8,128)(2,1)S(1)}, u32[]{:S(2)}, u32[]{:S(2)}) collective-permute-start(bf16[4,3,32,128]{3,2,1,0:T(8,128)(2,1)S(1)} %collective-permute-done.refs_1_), channel_id=1, source_target_pairs={{0,8},{8,0},{16,24},{24,16},{1,9},{9,1},{17,25},{25,17},{2,10},{10... | collective-permute-start | bytes 294920 | tf_op jit(solution)/shard_map/ppermute | solution.py:503
  17.0 0.1 collective-permute-start.3
  17.0 0.9 %collective-permute-done.2.refs_3_ = bf16[4,3,32,128]{3,2,1,0:T(8,128)(2,1)S(1)} collective-permute-done((bf16[4,3,32,128]{3,2,1,0:T(8,128)(2,1)S(1)}, bf16[4,3,32,128]{3,2,1,0:T(8,128)(2,1)S(1)}, u32[]{:S(2)}, u32[]{:S(2)}) %collective-permute-start.2) | collective-permute-done | bytes 98336 | tf_op jit(solution)/shard_map/ppermute | solution.py:503
  17.9 0.0 copy-start.3
  17.9 0.4 collective-permute-done.3.refs_4_
  18.3 0.0 copy-start.4
  18.3 0.0 copy-done.1
  18.3 0.0 copy-done.2
  18.3 0.3 copy-done.3
  18.5 0.4 copy-done.4
  18.9 22.9 %shard_map.119 = f32[3,4,8,128]{3,2,1,0:T(8,128)} custom-call(bf16[4,3,32,128]{3,2,1,0:T(8,128)(2,1)} %copy-done, bf16[4,3,32,128]{3,2,1,0:T(8,128)(2,1)} %copy-done.2, bf16[4,3,32,128]{3,2,1,0:T(8,128)(2,1)} %copy-done.1, bf16[4,3,32,128]{3,2,1,0:T(8,128)(2,1)} %copy-done.3, bf16[4,3,32,128]{3,2,1,0:T(8,128)(2,1)} %copy-done.4, ...), custom_call_target="tpu_custom_call" | custom-call | tf_op jit(solution)/shard_map/pallas_call | solution.py:556
Async XLA Ops:
  6.5 8.6 %copy-start = (bf16[4,3,32,128]{3,2,1,0:T(8,128)(2,1)}, bf16[4,3,32,128]{3,2,1,0:T(8,128)(2,1)S(1)}, u32[]{:S(2)}) copy-start(bf16[4,3,32,128]{3,2,1,0:T(8,128)(2,1)S(1)} %all_gather.3.refs_0_) | copy-start | bytes 294916
  6.5 8.6 %collective-permute-start.1 = (bf16[4,3,32,128]{3,2,1,0:T(8,128)(2,1)S(1)}, bf16[4,3,32,128]{3,2,1,0:T(8,128)(2,1)S(1)}, u32[]{:S(2)}, u32[]{:S(2)}) collective-permute-start(bf16[4,3,32,128]{3,2,1,0:T(8,128)(2,1)S(1)} %all_gather.3.refs_0_), channel_id=1, source_target_pairs={{6,0},{7,1},{0,2},{1,3},{2,4},{3,5},{4,6},{5,7},{10,8},{11,9},{12,... | collective-permute-start | bytes 294920 | tf_op jit(solution)/shard_map/ppermute | solution.py:500
  8.6 7.5 %collective-permute-start = (bf16[4,3,32,128]{3,2,1,0:T(8,128)(2,1)S(1)}, bf16[4,3,32,128]{3,2,1,0:T(8,128)(2,1)S(1)}, u32[]{:S(2)}, u32[]{:S(2)}) collective-permute-start(bf16[4,3,32,128]{3,2,1,0:T(8,128)(2,1)S(1)} %all_gather.3.refs_0_), channel_id=1, source_target_pairs={{7,0},{0,1},{1,2},{2,3},{3,4},{4,5},{5,6},{6,7},{9,8},{10,9},{11,1... | collective-permute-start | bytes 294920 | tf_op jit(solution)/shard_map/ppermute | solution.py:500
  15.2 3.1 %copy-start.1 = (bf16[4,3,32,128]{3,2,1,0:T(8,128)(2,1)}, bf16[4,3,32,128]{3,2,1,0:T(8,128)(2,1)S(1)}, u32[]{:S(2)}) copy-start(bf16[4,3,32,128]{3,2,1,0:T(8,128)(2,1)S(1)} %collective-permute-done.1.refs_2_) | copy-start | bytes 294916
  16.0 2.2 %copy-start.2 = (bf16[4,3,32,128]{3,2,1,0:T(8,128)(2,1)}, bf16[4,3,32,128]{3,2,1,0:T(8,128)(2,1)S(1)}, u32[]{:S(2)}) copy-start(bf16[4,3,32,128]{3,2,1,0:T(8,128)(2,1)S(1)} %collective-permute-done.refs_1_) | copy-start | bytes 294916
  16.0 1.9 %collective-permute-start.2 = (bf16[4,3,32,128]{3,2,1,0:T(8,128)(2,1)S(1)}, bf16[4,3,32,128]{3,2,1,0:T(8,128)(2,1)S(1)}, u32[]{:S(2)}, u32[]{:S(2)}) collective-permute-start(bf16[4,3,32,128]{3,2,1,0:T(8,128)(2,1)S(1)} %collective-permute-done.refs_1_), channel_id=1, source_target_pairs={{0,8},{8,0},{16,24},{24,16},{1,9},{9,1},{17,25},{25,17},{2,10},{10... | collective-permute-start | bytes 294920 | tf_op jit(solution)/shard_map/ppermute | solution.py:503
  17.0 1.3 %collective-permute-start.3 = (bf16[4,3,32,128]{3,2,1,0:T(8,128)(2,1)S(1)}, bf16[4,3,32,128]{3,2,1,0:T(8,128)(2,1)S(1)}, u32[]{:S(2)}, u32[]{:S(2)}) collective-permute-start(bf16[4,3,32,128]{3,2,1,0:T(8,128)(2,1)S(1)} %collective-permute-done.1.refs_2_), channel_id=1, source_target_pairs={{0,8},{8,0},{16,24},{24,16},{1,9},{9,1},{17,25},{25,17},{2,10},{10... | collective-permute-start | bytes 294920 | tf_op jit(solution)/shard_map/ppermute | solution.py:503
  17.9 0.6 %copy-start.3 = (bf16[4,3,32,128]{3,2,1,0:T(8,128)(2,1)}, bf16[4,3,32,128]{3,2,1,0:T(8,128)(2,1)S(1)}, u32[]{:S(2)}) copy-start(bf16[4,3,32,128]{3,2,1,0:T(8,128)(2,1)S(1)} %collective-permute-done.2.refs_3_) | copy-start | bytes 294916
  18.3 0.6 %copy-start.4 = (bf16[4,3,32,128]{3,2,1,0:T(8,128)(2,1)}, bf16[4,3,32,128]{3,2,1,0:T(8,128)(2,1)S(1)}, u32[]{:S(2)}) copy-start(bf16[4,3,32,128]{3,2,1,0:T(8,128)(2,1)S(1)} %collective-permute-done.3.refs_4_) | copy-start | bytes 294916
